TPU v7x, 512 devices: a whole 4x8x8 slice. The times are simulated.
512 devices in a mesh: ctx: 64 (over x, z, core), head: 8 (over y).
Axes of the slice: x: 4, y: 8, z: 8, core: 2. Of those that a mesh axis runs over, the one named last changes fastest.
Arguments:
- normed_query_latent: bfloat16 [2, 16, 1536], replicated, may hold values from -48 to 48
- fresh_token_latent: bfloat16 [2, 16, 576], replicated, may hold values from -16 to 16
- prefix_latent_cache: bfloat16 [32768, 576], P('ctx'), may hold values from -18 to 18
- query_up_weight: bfloat16 [1536, 24576], P(None, ('head', 'ctx')), may hold values from -0.15625 to 0.15625
- key_up_weight: bfloat16 [128, 128, 512], P('head', None, 'ctx'), may hold values from -0.5 to 0.5
- value_up_weight: bfloat16 [128, 512, 128], P('head', 'ctx'), may hold values from -0.25 to 0.25
- output_weight: bfloat16 [16384, 7168], P('head', 'ctx'), may hold values from -0.046875 to 0.046875
- adapter_query_down: bfloat16 [8, 1536, 16], replicated, may hold values from -0.15625 to 0.15625
- adapter_query_up: bfloat16 [8, 16, 24576], P(None, None, ('head', 'ctx')), may hold values from -1.5 to 1.5
- adapter_key_down: bfloat16 [8, 512, 16], P(None, 'ctx'), may hold values from -1.5 to 1.5
- adapter_key_up: bfloat16 [8, 16, 16384], P(None, None, 'head'), may hold values from -0.5 to 0.5
- adapter_value_down: bfloat16 [8, 512, 16], P(None, 'ctx'), may hold values from -0.25 to 0.25
- adapter_value_up: bfloat16 [8, 16, 16384], P(None, None, 'head'), may hold values from -1.5 to 1.5
- request_adapter: int32 [16], replicated, may hold values from 0 to 7, as said below
- group_first_request: int32 [8], replicated, may hold values from 0 to 15, as said below
- group_request_count: int32 [8], replicated, may hold values from 1 to 8, as said below
Outputs:
- mixed: bfloat16 [16, 2, 7168], P('head', None, 'ctx')
Inputs may be any that keep to these rules, and one draw needn't show every extreme that they name: Requests come ordered by adapter: request_adapter never falls, and the requests of adapter a are exactly rows group_first_request[a] to group_first_request[a] + group_request_count[a] - 1. group_first_request[a] is the number of requests whose adapter is below a. `group_request_count`: every adapter has at least one request; some adapter has exactly 8 in every draw; the counts sum to 16.
All inputs are finite; a program needn't handle non-finite values.
Results may differ from a plain program's by a relative error of at most 0.022.
The roundings to bfloat16 on the way count: a program that leaves them out, or rounds other values in their place, can miss the bound.
Values may be sent and summed in bfloat16 or wider, within the bound.
A program may use at most 128 MiB of HBM per device.

v0:
```python
import math

import jax
import jax.numpy as jnp
from jax import lax
from jax.sharding import PartitionSpec as P

NOPE_WIDTH = 128
ROPE_WIDTH = 64
CAP = 8


def combined_all(shard, axis, combine):
    everything = jax.tree.map(lambda part: lax.all_gather(part, axis), shard)
    leading = jax.tree.map(lambda part: part[0], everything)

    def lap(k, so_far):
        return combine(so_far, jax.tree.map(lambda part: part[k], everything))

    return lax.fori_loop(1, lax.axis_size(axis), lap, leading)


def slot_places(request_adapter, group_first_request, group_request_count, capacity):
    adapter_list = group_first_request.shape[0]
    adapter_indicator = (
        request_adapter[:, None] == jnp.arange(adapter_list, dtype=jnp.int32)[None, :]
    )
    own_start = jnp.sum(jnp.where(adapter_indicator, group_first_request[None, :], 0), axis=1)
    own_count = jnp.sum(jnp.where(adapter_indicator, group_request_count[None, :], 0), axis=1)
    within = jnp.arange(request_adapter.shape[0], dtype=jnp.int32) - own_start
    is_live = jnp.logical_and(within >= 0, within < own_count)
    slot_index = request_adapter * capacity + jnp.clip(within, 0, capacity - 1)
    return (adapter_indicator, slot_index, is_live)


def padded_rows(values, group_first_request, capacity):
    steps_n = values.shape[0]
    padding_rows = jnp.zeros((steps_n, capacity) + values.shape[2:], values.dtype)
    extended = jnp.concatenate([values, padding_rows], axis=1)
    pick_rows = (
        group_first_request[:, None] + jnp.arange(capacity, dtype=jnp.int32)[None, :]
    ).reshape(-1)
    gathered = jnp.take(extended, pick_rows, axis=1)
    return gathered.reshape((steps_n, group_first_request.shape[0], capacity) + values.shape[2:])


def back_to_requests(padded, slot_index, is_live):
    steps_n = padded.shape[0]
    merged_slots = padded.reshape((steps_n, -1) + padded.shape[3:])
    request_rows = jnp.take(merged_slots, slot_index, axis=1)
    live_mask = is_live.reshape((1, -1) + (1,) * (request_rows.ndim - 2))
    return jnp.where(live_mask, request_rows, jnp.zeros_like(request_rows))


def spread_rank(low_rank, adapter_indicator):
    adapter_list = adapter_indicator.shape[1]
    extra_dims = low_rank.ndim - 3
    mask_shape = (1, adapter_indicator.shape[0]) + (1,) * extra_dims + (adapter_list, 1)
    placed = jnp.where(
        adapter_indicator.reshape(mask_shape), low_rank[..., None, :], jnp.zeros((), low_rank.dtype)
    )
    return placed.reshape(low_rank.shape[:-1] + (adapter_list * low_rank.shape[-1],))


def absorb_weights(query_unrotated, reduced_key, key_up, key_down, adapter_indicator):
    adapter_list, channels, rank_length = key_down.shape
    key_adapter_table = jnp.transpose(key_down, (0, 2, 1)).reshape(
        adapter_list * rank_length, channels
    )
    base_scores = jnp.einsum(
        "srhd,hdl->srhl", query_unrotated, key_up, preferred_element_type=jnp.float32
    )
    adapter_scores = jnp.einsum(
        "srhj,jl->srhl",
        spread_rank(reduced_key, adapter_indicator),
        key_adapter_table,
        preferred_element_type=jnp.float32,
    )
    return (base_scores + adapter_scores).astype(jnp.bfloat16)


def combine(earlier, later):
    max_first, total_first, value_first, low_first = earlier
    max_second, total_second, value_second, low_second = later
    joined = jnp.maximum(max_first, max_second)
    factor_first = jnp.exp(max_first - joined)
    factor_second = jnp.exp(max_second - joined)
    row_total = total_first * factor_first + total_second * factor_second
    value_sum = value_first * factor_first[..., None] + value_second * factor_second[..., None]
    low_sum = low_first * factor_first[..., None] + low_second * factor_second[..., None]
    return (joined, row_total, value_sum, low_sum)


def body(
    normed_query_latent,
    fresh_token_latent,
    prefix_latent_cache,
    query_up_weight,
    key_up_weight,
    value_up_weight,
    output_weight,
    adapter_query_down,
    adapter_query_up,
    adapter_key_down,
    adapter_key_up,
    adapter_value_down,
    adapter_value_up,
    request_adapter,
    group_first_request,
    group_request_count,
):
    steps_n, request_n, _ = normed_query_latent.shape
    adapter_list = adapter_query_down.shape[0]
    rank_length = adapter_query_down.shape[2]
    capacity = CAP
    head_width = NOPE_WIDTH + ROPE_WIDTH
    adapter_indicator, slot_index, is_live = slot_places(
        request_adapter, group_first_request, group_request_count, capacity
    )
    latent_zero_fill = padded_rows(normed_query_latent, group_first_request, capacity)
    reduced_query = jnp.einsum(
        "pmvx,mxe->pmve", latent_zero_fill, adapter_query_down, preferred_element_type=jnp.float32
    ).astype(jnp.bfloat16)
    reduced_query = back_to_requests(reduced_query, slot_index, is_live)
    query_adapter_table = adapter_query_up.reshape(
        adapter_list * rank_length, adapter_query_up.shape[2]
    )
    query_cols = jnp.einsum(
        "srq,qc->src", normed_query_latent, query_up_weight, preferred_element_type=jnp.float32
    )
    query_cols = query_cols + jnp.einsum(
        "srj,jc->src",
        spread_rank(reduced_query, adapter_indicator),
        query_adapter_table,
        preferred_element_type=jnp.float32,
    )
    query_cols = query_cols.astype(jnp.bfloat16)
    queries = lax.all_gather(query_cols, "ctx", axis=2, tiled=True)
    device_heads = queries.shape[2] // head_width
    queries = queries.reshape(steps_n, request_n, device_heads, head_width)
    query_unrotated = queries[..., :NOPE_WIDTH]
    query_pe = queries[..., NOPE_WIDTH:]
    nope_pad = padded_rows(query_unrotated, group_first_request, capacity)
    key_adapter_factor = adapter_key_up.reshape(adapter_list, rank_length, device_heads, NOPE_WIDTH)
    reduced_key = jnp.einsum(
        "sachd,akhd->sachk", nope_pad, key_adapter_factor, preferred_element_type=jnp.float32
    ).astype(jnp.bfloat16)
    reduced_key = back_to_requests(reduced_key, slot_index, is_live)
    latent_scores = absorb_weights(
        query_unrotated, reduced_key, key_up_weight, adapter_key_down, adapter_indicator
    )
    latent_queries = lax.all_gather(latent_scores, "ctx", axis=3, tiled=True)
    value_up, value_down = (
        lax.all_gather(value_up_weight, "ctx", axis=1, tiled=True),
        lax.all_gather(adapter_value_down, "ctx", axis=1, tiled=True),
    )
    latent_width = latent_queries.shape[3]
    joined_query = jnp.concatenate([latent_queries, query_pe], axis=3)
    cache_lat = prefix_latent_cache[:, :latent_width]
    new_lat = fresh_token_latent[..., :latent_width]
    score_scale = 1.0 / math.sqrt(head_width)
    scores = (
        jnp.einsum(
            "srhc,jc->srhj", joined_query, prefix_latent_cache, preferred_element_type=jnp.float32
        )
        * score_scale
    )
    own_scores = (
        jnp.einsum(
            "srhc,trc->srht", joined_query, fresh_token_latent, preferred_element_type=jnp.float32
        )
        * score_scale
    )
    step_ids = jnp.arange(steps_n, dtype=jnp.int32)
    causal = step_ids[None, :] <= step_ids[:, None]
    holds_own = jnp.logical_and(causal, lax.axis_index("ctx") == 0)
    own_scores = jnp.where(holds_own[:, None, None, :], own_scores, -jnp.inf)
    row_max = jnp.maximum(jnp.max(scores, axis=3), jnp.max(own_scores, axis=3))
    weights = jnp.exp(scores - row_max[..., None])
    own_weights = jnp.exp(own_scores - row_max[..., None])
    row_total = jnp.sum(weights, axis=3) + jnp.sum(own_weights, axis=3)
    latent_sum = jnp.einsum(
        "srhj,jl->srhl", weights.astype(jnp.bfloat16), cache_lat, preferred_element_type=jnp.float32
    )
    latent_sum = latent_sum + jnp.einsum(
        "srht,trl->srhl",
        own_weights.astype(jnp.bfloat16),
        new_lat,
        preferred_element_type=jnp.float32,
    )
    value_part = jnp.einsum(
        "srhl,hlv->srhv", latent_sum, value_up.astype(jnp.float32), precision=lax.Precision.HIGHEST
    )
    down_factor_rows = jnp.take(value_down, request_adapter, axis=0).astype(jnp.float32)
    low_part = jnp.einsum(
        "srhl,rlk->srhk", latent_sum, down_factor_rows, precision=lax.Precision.HIGHEST
    )
    row_max, row_total, value_sum, low_sum = combined_all(
        (row_max, row_total, value_part, low_part), "ctx", combine
    )
    value_out = value_sum / row_total[..., None]
    low_value = (low_sum / row_total[..., None]).astype(jnp.bfloat16)
    value_adapter_table = adapter_value_up.reshape(
        adapter_list * rank_length, device_heads, adapter_value_up.shape[2] // device_heads
    )
    value_delta = jnp.einsum(
        "srhj,jhv->srhv",
        spread_rank(low_value, adapter_indicator),
        value_adapter_table,
        preferred_element_type=jnp.float32,
    )
    attention = (value_out + value_delta).astype(jnp.bfloat16).reshape(steps_n, request_n, -1)
    mixed = lax.psum_scatter(
        jnp.einsum("srf,fd->rsd", attention, output_weight, preferred_element_type=jnp.float32),
        "head",
        scatter_dimension=0,
        tiled=True,
    )
    return mixed.astype(jnp.bfloat16)


def solution(mesh):
    placed = (
        P(),
        P(),
        P("ctx", None),
        P(None, ("head", "ctx")),
        P("head", None, "ctx"),
        P("head", "ctx", None),
        P("head", "ctx"),
        P(),
        P(None, None, ("head", "ctx")),
        P(None, "ctx", None),
        P(None, None, "head"),
        P(None, "ctx", None),
        P(None, None, "head"),
        P(),
        P(),
        P(),
    )
    return jax.shard_map(
        body, mesh=mesh, in_specs=placed, out_specs=P("head", None, "ctx"), check_vma=False
    )
```

profile of v0, /device:TPU:1, one launch (start us, length us, event | category | flops | bytes accessed | tf_op | source)
XLA Modules:
  0.0 667.7 jit_solution(2725192231798893893)
XLA Ops:
  10.4 1.0 copy.196
  12.2 1.4 gather_fusion
  13.6 1.3 fusion.29
  15.8 1.0 convolution_bitcast_fusion.4
  16.9 1.1 fusion.32
  18.1 58.1 %all_gather.32 = bf16[2,16,3072]{1,0,2:T(2,128)(2,1)S(1)} all-gather(bf16[2,16,48]{1,0,2:T(2,128)(2,1)S(1)} %copy.201), channel_id=1, replica_groups=mesh['ctx'=64,'head'=8] {'ctx'}, dimensions={2}, use_global_device_ids=true | all-gather | bytes 199680 | tf_op jit(solution)/shard_map/all_gather | solution.py:138
  80.1 1.8 convolution_bitcast_fusion.2
  82.3 55.9 %all_gather.33 = bf16[2,16,16,512]{1,3,0,2:T(8,128)(2,1)S(1)} all-gather(bf16[2,16,16,8]{1,3,0,2:T(8,128)(2,1)S(1)} %fusion.28), channel_id=1, replica_groups=mesh['ctx'=64,'head'=8] {'ctx'}, dimensions={3}, use_global_device_ids=true | all-gather | bytes 532480 | tf_op jit(solution)/shard_map/all_gather | solution.py:152
  138.3 2.7 constant_dynamic-update-slice_fusion
  142.0 3.9 copy.212
  145.9 1.0 fusion.83
  147.1 3.8 fusion.82
  151.0 48.6 %all_gather.39 = bf16[8,512,16]{2,1,0:T(8,128)(2,1)S(1)} all-gather(bf16[8,8,16]{2,1,0:T(8,128)(2,1)S(1)} %copy-done.6), channel_id=1, replica_groups=mesh['ctx'=64,'head'=8] {'ctx'}, dimensions={1}, use_global_device_ids=true | all-gather | bytes 133120 | tf_op jit(solution)/shard_map/all_gather | solution.py:155
  199.7 2.2 gather_fusion.4
  203.4 3.0 fusion.22
  206.5 3.8 fusion.19
  210.6 50.0 %all-gather.1 = f32[128,16,16]{2,1,0:T(8,128)S(1)} all-gather(f32[2,16,16]{2,1,0:T(8,128)S(1)} %copy.218), channel_id=3, replica_groups=mesh['ctx'=64,'head'=8] {'ctx'}, dimensions={0}, use_global_device_ids=true | all-gather | bytes 133120 | tf_op jit(solution)/shard_map/all_gather | solution.py:14
  260.6 52.9 %all-gather = f32[128,16,16]{2,1,0:T(8,128)} all-gather(f32[2,16,16]{2,1,0:T(8,128)S(1)} %copy.215), channel_id=2, replica_groups=mesh['ctx'=64,'head'=8] {'ctx'}, dimensions={0}, use_global_device_ids=true | all-gather | bytes 133120 | tf_op jit(solution)/shard_map/all_gather | solution.py:14
  314.6 1.4 dynamic-slice
  317.8 100.1 %all-gather.10.cloned.1.call-done = f32[128,16,16,128]{3,1,0,2:T(8,128)} async-done(((f32[2,16,16,128]{3,1,0,2:T(8,128)}), f32[128,16,16,128]{3,1,0,2:T(8,128)}) %all-gather.10.cloned.1.call-update) | async-done | bytes 16777232 | tf_op jit(solution)/shard_map/all_gather | solution.py:14
  419.0 217.2 %while.21 = (s32[]{:T(128)}, f32[2,16,16]{2,1,0:T(8,128)S(1)}, f32[2,16,16]{2,1,0:T(8,128)S(1)}, f32[2,16,16,128]{3,2,1,0:T(8,128)S(1)}, f32[2,16,16,16]{3,2,1,0...) while((s32[]{:T(128)}, f32[2,16,16]{2,1,0:T(8,128)S(1)}, ...), condition=%wide.region_7.8_spmd, body=%wide.region_6.7_spmd.sunk | while | flops 224261 | bytes 1564843 | solution.py:20
  421.1 1.0 constant_dynamic-slice_fusion.4
  424.6 1.0 constant_dynamic-slice_fusion.4
  428.0 1.0 constant_dynamic-slice_fusion.4
  431.5 1.0 constant_dynamic-slice_fusion.4
  434.9 1.0 constant_dynamic-slice_fusion.4
  438.4 1.0 constant_dynamic-slice_fusion.4
  441.8 1.0 constant_dynamic-slice_fusion.4
  445.2 1.0 constant_dynamic-slice_fusion.4
  448.7 1.0 constant_dynamic-slice_fusion.4
  452.1 1.0 constant_dynamic-slice_fusion.4
  472.8 1.0 constant_dynamic-slice_fusion.4
  476.3 1.0 constant_dynamic-slice_fusion.4
  479.7 1.0 constant_dynamic-slice_fusion.4
  503.8 1.0 constant_dynamic-slice_fusion.4
  507.3 1.0 constant_dynamic-slice_fusion.4
  510.7 1.0 constant_dynamic-slice_fusion.4
  538.3 1.0 constant_dynamic-slice_fusion.4
  541.8 1.0 constant_dynamic-slice_fusion.4
  545.2 1.0 constant_dynamic-slice_fusion.4
  569.3 1.0 constant_dynamic-slice_fusion.4
  572.8 1.0 constant_dynamic-slice_fusion.4
  576.2 1.0 constant_dynamic-slice_fusion.4
  603.8 1.0 constant_dynamic-slice_fusion.4
  607.3 1.0 constant_dynamic-slice_fusion.4
  610.7 1.0 constant_dynamic-slice_fusion.4
  634.8 1.0 constant_dynamic-slice_fusion.4
  637.8 22.7 %all-reduce.2 = bf16[16,2,112]{2,0,1:T(8,128)(2,1)S(1)} all-reduce(f32[16,2,112]{2,0,1:T(8,128)S(1)} %convolution_bitcast_fusion.5), channel_id=6, replica_groups=mesh['ctx'=64,'head'=8] {'head'}, use_global_device_ids=true, to_apply=%region_8.9.clone | all-reduce | flops 3584 | bytes 21504
  (442 shorter events, 207.3 us)
Async XLA Ops:
  6.5 631.1 %copy-start = (bf16[2048,112]{0,1:T(8,128)(2,1)S(1)}, bf16[2048,112]{0,1:T(8,128)(2,1)}, u32[]{:S(2)}) copy-start(bf16[2048,112]{0,1:T(8,128)(2,1)} %param.24) | copy-start | bytes 1376260
  6.5 200.0 %all-gather.8.cloned.1.call-start = ((), (), s32[]{:S(2)}) async-start(), calls=%async_computation | async-start | bytes 2129920 | tf_op jit(solution)/shard_map/all_gather | solution.py:154
  7.3 309.4 %all-gather.12.cloned.1.call-start = ((), (), s32[]{:S(2)}) async-start(), calls=%async_computation.2 | async-start | bytes 17039360 | tf_op jit(solution)/shard_map/all_gather | solution.py:14
  15.0 63.7 %copy-start.3 = (bf16[8,16,2048]{2,1,0:T(8,128)(2,1)S(1)}, bf16[8,16,2048]{2,1,0:T(8,128)(2,1)}, u32[]{:S(2)}) copy-start(bf16[8,16,2048]{2,1,0:T(8,128)(2,1)} %param.28) | copy-start | bytes 1572868
  76.9 3.1 copy-start.9
  78.0 4.1 copy-start.8
  141.0 4.9 copy-start.5
  141.0 6.1 copy-start.1
  145.9 5.1 copy-start.6
  145.9 53.7 %copy-start.7 = (s32[16]{0:T(128)S(1)}, s32[16]{0:T(128)}, u32[]{:S(2)}) copy-start(s32[16]{0:T(128)} %param.31) | copy-start | bytes 196
  201.8 1.6 copy-start.2
  206.4 108.0 %copy-start.4 = (bf16[8,16,2048]{2,1,0:T(8,128)(2,1)S(1)}, bf16[8,16,2048]{2,1,0:T(8,128)(2,1)}, u32[]{:S(2)}) copy-start(bf16[8,16,2048]{2,1,0:T(8,128)(2,1)} %param.30) | copy-start | bytes 1572868
  206.4 211.4 %all-gather.10.cloned.1.call-start = ((), (), s32[]{:S(2)}) async-start(), calls=%async_computation.1 | async-start | bytes 17039360 | tf_op jit(solution)/shard_map/all_gather | solution.py:14
Sparse Core Ops, SparseCore 0:
  10.5 84.3 all-gather.7
  206.6 105.3 all-gather.11
  315.3 102.4 all-gather.9
where the time goes:
time: 680 us; the launch traced here: 668 us
  blocking collectives  288 us (42%)
  local copies, waits for them, and re-layouts  155 us (23%)
  waiting for transfers between devices  101 us (15%)
  other arithmetic  87.2 us (13%)
  matrix products  19.1 us (3%)
  between operations  14.2 us (2%)
    dynamic_slice x189, local copies, waits for them, and re-layouts, lap(): return combine(so_far, jax.tree.map(lambda part: part[k], everything))  132 us
    all_gather x2, blocking collectives, combined_all(): everything = jax.tree.map(lambda part: lax.all_gather(part, axis), shard)  103 us
    all_gather x2, waiting for transfers between devices, combined_all(): everything = jax.tree.map(lambda part: lax.all_gather(part, axis), shard)  100 us
    all_gather x1, blocking collectives, body(): queries = lax.all_gather(query_cols, 'ctx', axis=2, tiled=True)  58.1 us
    all_gather x1, blocking collectives, body(): latent_queries = lax.all_gather(latent_scores, 'ctx', axis=3, tiled=True)  55.9 us
    all_gather x1, blocking collectives, body(): lax.all_gather(adapter_value_down, 'ctx', axis=1, tiled=True)  48.6 us
    add x63, other arithmetic, combine(): row_total = total_first * factor_first + total_second * factor_second  46.8 us
    unnamed x1, blocking collectives  22.7 us
  transfers between devices with their start and end apart: 3, of which 1 were waited for; matrix products, arithmetic and copies ran while one was open for 6% of the time, Pallas kernels for 0%

commit v1 on v0

v1 whole, which is shorter than its diff:
```python
import functools
import math

import jax
import jax.numpy as jnp
from jax import lax
from jax.experimental import pallas as pl
from jax.experimental.pallas import tpu as pltpu
from jax.sharding import PartitionSpec as P

MESH = pl.DeviceIdType.MESH
F32 = jnp.float32
BF16 = jnp.bfloat16

CTX = 64
CHIPS = CTX // 2
GROUPS = 8
HEADS = 16
HALF = HEADS // 2
ROWS = 32
REQ = 16
NOPE = 128
ROPE = 64
LAT = 512
COLS = 48
KEYS = 512
WIDTH = 112
SCALE = 1.0 / math.sqrt(NOPE + ROPE)


def mm(a, b):
    return lax.dot_general(a, b, (((1,), (0,)), ((), ())), preferred_element_type=F32)


def mm_t(a, b):
    return lax.dot_general(a, b, (((1,), (1,)), ((), ())), preferred_element_type=F32)


def kernel(
    x_hbm,
    fresh_hbm,
    cache_hbm,
    wq_hbm,
    kup_hbm,
    vup_hbm,
    wo_hbm,
    aqd_hbm,
    aqu_hbm,
    akd_hbm,
    aku_hbm,
    avd_hbm,
    avu_hbm,
    adapter_s,
    first_s,
    count_s,
    out_ref,
    x_v,
    fresh_v,
    cache_v,
    wq_v,
    kup_v,
    vup_v,
    wo_v,
    aqd_v,
    aqu_v,
    akd_v,
    aku_v,
    avd_v,
    avu_v,
    kmsg,
    vmsg,
    kw,
    vw,
    qcol,
    lq_s,
    pe_s,
    lat,
    pos,
    acc_s,
    acc_r,
    ml_s,
    ml_r,
    turned,
    live_mask,
    own_mask,
    att,
    part,
    part_r,
    load_sem,
    send_sem,
    recv_sem,
):
    me = lax.axis_index("ctx")
    group = lax.axis_index("head")
    chip = me // 2
    core = me % 2
    head_up = me // 4
    quarter = me % 4
    up_core = head_up // HALF
    head_own = core * HALF + chip // 4
    block = chip % 4

    barrier = pltpu.get_barrier_semaphore()

    def greet(k, carry):
        pl.semaphore_signal(
            barrier, inc=1, device_id=((me + k) % CTX, group), device_id_type=MESH
        )
        return carry

    lax.fori_loop(1, CTX, greet, 0)

    def greet_group(k, carry):
        pl.semaphore_signal(
            barrier, inc=1, device_id=(me, (group + k) % GROUPS), device_id_type=MESH
        )
        return carry

    lax.fori_loop(1, GROUPS, greet_group, 0)

    up_col = pl.multiple_of(head_up * NOPE, NOPE)
    own_col = pl.multiple_of(head_own * NOPE, NOPE)
    loads = [
        pltpu.make_async_copy(src, dst, load_sem.at[n])
        for n, (src, dst) in enumerate(
            (
                (kup_hbm, kup_v),
                (akd_hbm, akd_v),
                (x_hbm, x_v),
                (aqd_hbm, aqd_v),
                (wq_hbm, wq_v),
                (aqu_hbm, aqu_v),
                (vup_hbm, vup_v),
                (avd_hbm, avd_v),
                (aku_hbm.at[:, pl.ds(up_col, NOPE)], aku_v),
                (cache_hbm, cache_v.at[0]),
                (fresh_hbm, fresh_v),
                (avu_hbm.at[:, pl.ds(own_col, NOPE)], avu_v),
                (wo_hbm, wo_v),
            )
        )
    ]
    for load in loads:
        load.start()
    (
        kup_l,
        akd_l,
        x_l,
        aqd_l,
        wq_l,
        aqu_l,
        vup_l,
        avd_l,
        aku_l,
        cache_l,
        fresh_l,
        avu_l,
        wo_l,
    ) = loads

    lane_adapter = lax.broadcasted_iota(jnp.int32, (ROWS, 128), 1) // 16
    row_request = lax.broadcasted_iota(jnp.int32, (ROWS, 128), 0) % REQ
    adapter = jnp.zeros((ROWS, 128), jnp.int32)
    first = jnp.zeros((ROWS, 128), jnp.int32)
    count = jnp.zeros((ROWS, 128), jnp.int32)
    for r in range(REQ):
        adapter = jnp.where(row_request == r, adapter_s[r], adapter)
    for a in range(8):
        first = jnp.where(lane_adapter == a, first_s[a], first)
        count = jnp.where(lane_adapter == a, count_s[a], count)
    owns = adapter == lane_adapter
    within = row_request - first
    live = jnp.logical_and(owns, jnp.logical_and(within >= 0, within < count))
    own_mask[...] = jnp.where(owns, 1.0, 0.0).astype(F32)
    live_mask[...] = jnp.where(live, 1.0, 0.0).astype(F32)

    kup_l.wait()
    akd_l.wait()
    table = jnp.concatenate([akd_v[a].astype(F32) for a in range(8)], axis=1)
    for h in range(HEADS):
        kmsg[h] = jnp.concatenate([kup_v[h].astype(F32), table], axis=0).astype(BF16)

    pl.semaphore_wait(barrier, CTX - 1 + GROUPS - 1)

    def send(src, dst, n, ctx, y):
        return pltpu.make_async_remote_copy(
            src_ref=src,
            dst_ref=dst,
            send_sem=send_sem.at[n],
            recv_sem=recv_sem.at[n],
            device_id=(ctx, y),
            device_id_type=MESH,
        )

    def arrived(ref, n):
        pltpu.make_async_copy(ref, ref, recv_sem.at[n]).wait()

    def sent(ref, n):
        pltpu.make_async_copy(ref, ref, send_sem.at[n]).wait()

    def send_or_keep(src, dst, n, ctx):
        @pl.when(ctx == me)
        def _():
            pltpu.make_async_copy(src, dst, recv_sem.at[n]).start()

        @pl.when(ctx != me)
        def _():
            send(src, dst, n, ctx, group).start()

    def send_keys(k, carry):
        h = (head_up + k) % HEADS
        send_or_keep(kmsg.at[h], kw.at[me % 16], 0, 4 * h + me // 16)
        return carry

    lax.fori_loop(0, HEADS, send_keys, 0)

    sibling = 2 * chip + 1 - core
    share = send(cache_hbm, cache_v.at[1], 1, sibling, group)
    share.start()

    x_l.wait()
    aqd_l.wait()
    x = x_v[...]
    low = (mm_t(x, aqd_v[...]) * live_mask[...]).astype(BF16)
    wq_l.wait()
    aqu_l.wait()
    cols = (mm_t(x, wq_v[...]) + mm(low, aqu_v[...])).astype(BF16)
    qcol[quarter] = jnp.concatenate(
        [cols.astype(F32), jnp.zeros((ROWS, 128 - COLS), F32)], axis=1
    ).astype(BF16)

    for k in range(1, 4):
        send(
            qcol.at[quarter],
            qcol.at[quarter],
            2,
            4 * head_up + (quarter + k) % 4,
            group,
        ).start()

    vup_l.wait()
    avd_l.wait()
    table = jnp.concatenate([avd_v[a].astype(F32) for a in range(8)], axis=1)
    for h in range(HEADS):
        vmsg[h] = jnp.concatenate([vup_v[h].astype(F32), table], axis=0).astype(BF16)

    def send_values(k, carry):
        dest = (me + k) % CTX
        h = HALF * (dest % 2) + dest // 8
        send_or_keep(vmsg.at[h], vw.at[me], 3, dest)
        return carry

    arrived(qcol.at[pl.ds(0, 3)], 2)
    q0 = qcol[0].astype(F32)
    q1 = qcol[1].astype(F32)
    q2 = qcol[2].astype(F32)
    q3 = qcol[3].astype(F32)
    nope = jnp.concatenate([q0[:, :48], q1[:, :48], q2[:, :32]], axis=1).astype(BF16)
    pe = jnp.concatenate([q2[:, 32:48], q3[:, :48]], axis=1)
    pe_s[...] = jnp.concatenate([pe[:16], pe[16:]], axis=1).astype(BF16)

    def send_pe(k, carry):
        there = 4 * ((chip // 4 + k) % 8) + quarter
        send_or_keep(pe_s, pos.at[head_up % HALF], 4, 2 * there + up_core)
        return carry

    lax.fori_loop(0, 8, send_pe, 0)

    aku_l.wait()
    low_key = (mm_t(nope, aku_v[...]) * live_mask[...]).astype(BF16)
    arrived(kw, 0)
    kwf = kw[...].astype(F32)
    key_up = kwf[:, :8].reshape(128, 128).astype(BF16)
    key_down = kwf[:, 8:].reshape(128, 128).astype(BF16)
    lq_s[...] = (mm_t(nope, key_up) + mm_t(low_key, key_down)).astype(BF16)

    slot = (head_up % HALF) * 4 + quarter

    def send_lat(k, carry):
        there = (chip + k) % CHIPS
        send_or_keep(lq_s, lat.at[slot], 5, 2 * there + up_core)
        return carry

    lax.fori_loop(0, CHIPS, send_lat, 0)
    lax.fori_loop(0, CTX, send_values, 0)

    arrived(pos, 4)
    arrived(lat, 5)
    q_lat = jnp.concatenate(
        [
            jnp.concatenate([lat[4 * h + j] for j in range(4)], axis=1)
            for h in range(HALF)
        ],
        axis=0,
    )
    both = pos[...].astype(F32)
    q_pe = (
        jnp.concatenate([both[:, :, :ROPE], both[:, :, ROPE:]], axis=1)
        .reshape(HALF * ROWS, ROPE)
        .astype(BF16)
    )
    cache_l.wait()
    share.wait_recv()
    scores = [
        (mm(q_lat, cache_v[n, :LAT]) + mm(q_pe, cache_v[n, LAT:])) * SCALE
        for n in range(2)
    ]
    top = jnp.maximum(
        jnp.max(scores[0], axis=1, keepdims=True),
        jnp.max(scores[1], axis=1, keepdims=True),
    )
    weights = [jnp.exp(s - top) for s in scores]
    total = jnp.sum(weights[0], axis=1, keepdims=True) + jnp.sum(
        weights[1], axis=1, keepdims=True
    )
    lane = lax.broadcasted_iota(jnp.int32, (HALF * ROWS, 128), 1)
    stats = jnp.where(lane == 0, top, jnp.where(lane == 1, total, 0.0))
    stats = stats.T
    for half in range(2):
        ml_s[half] = stats[0:2, 128 * half : 128 * half + 128]

    def send_stats(k, carry):
        there = (chip + k) % CHIPS
        send(ml_s.at[there // 16], ml_r.at[chip], 6, 2 * there + core, group).start()
        return carry

    lax.fori_loop(1, CHIPS, send_stats, 0)
    pltpu.make_async_copy(ml_s.at[chip // 16], ml_r.at[chip], recv_sem.at[6]).start()

    summed = sum(
        mm_t(weights[n].astype(BF16), cache_v[n, :LAT]) for n in range(2)
    )
    for pair in range(2):
        low_half = summed[:, 256 * pair : 256 * pair + 128].reshape(CHIPS, 8, 128)
        high_half = summed[:, 256 * pair + 128 : 256 * pair + 256].reshape(
            CHIPS, 8, 128
        )
        acc_s[:, 16 * pair : 16 * pair + 16] = jnp.concatenate(
            [low_half, high_half], axis=1
        ).astype(BF16)

    def send_acc(k, carry):
        there = (chip + k) % CHIPS
        send(acc_s.at[there], acc_r.at[chip], 7, 2 * there + core, group).start()
        return carry

    lax.fori_loop(1, CHIPS, send_acc, 0)
    pltpu.make_async_copy(acc_s.at[chip], acc_r.at[chip], recv_sem.at[7]).start()

    fresh_l.wait()
    fresh = fresh_v[...]
    own_head = (chip // 4) * 4
    own_lat = jnp.concatenate([lat[own_head + j] for j in range(4)], axis=1)
    both = pos[chip // 4].astype(F32)
    own_pe = jnp.concatenate([both[:, :ROPE], both[:, ROPE:]], axis=0).astype(BF16)
    own_scores = (mm_t(own_lat, fresh[:, :LAT]) + mm_t(own_pe, fresh[:, LAT:])) * SCALE
    row = lax.broadcasted_iota(jnp.int32, (ROWS, ROWS), 0)
    key = lax.broadcasted_iota(jnp.int32, (ROWS, ROWS), 1)
    seen = jnp.logical_and(row % REQ == key % REQ, key // REQ <= row // REQ)
    own_scores = jnp.where(seen, own_scores, -jnp.inf)
    own_top = jnp.max(own_scores, axis=1, keepdims=True)
    own_weights = jnp.exp(own_scores - own_top)
    own_total = jnp.sum(own_weights, axis=1, keepdims=True)
    own_sum = mm(own_weights.astype(BF16), fresh[:, :LAT])

    def mine(a):
        rows = [a[8 * b : 8 * b + 8] for b in range(4)]
        low_pair = jnp.where(block == 0, rows[0], rows[1])
        high_pair = jnp.where(block == 2, rows[2], rows[3])
        return jnp.where(block < 2, low_pair, high_pair)

    own_top = mine(own_top)
    own_total = mine(own_total)
    own_sum = mine(own_sum)
    mask = mine(own_mask[...])

    arrived(vw, 3)
    vwf = vw[...].astype(F32)
    value_up = vwf[:, :8].reshape(LAT, 128).astype(BF16)
    value_down = vwf[:, 8:].reshape(LAT, 128).astype(BF16)

    arrived(ml_r, 6)
    ml = ml_r[...]
    turned[...] = jnp.concatenate(
        [ml[:, 0], ml[:, 1], jnp.zeros((64, 128), F32)], axis=0
    ).T
    stats = turned[pl.ds(pl.multiple_of(8 * (chip % 16), 8), 8), :]
    tops = stats[:, :CHIPS]
    totals = stats[:, CHIPS : 2 * CHIPS]
    joined = jnp.maximum(jnp.max(tops, axis=1, keepdims=True), own_top)
    factors = jnp.exp(tops - joined)
    own_factor = jnp.exp(own_top - joined)
    row_total = (
        jnp.sum(factors * totals, axis=1, keepdims=True) + own_factor * own_total
    )
    arrived(acc_r, 7)
    latent = own_sum * own_factor
    latent = [latent[:, 128 * j : 128 * j + 128] for j in range(4)]
    for n in range(CHIPS):
        factor = factors[:, n : n + 1]
        got = acc_r[n].astype(F32)
        for j in range(4):
            latent[j] = latent[j] + factor * got[8 * j : 8 * j + 8]
    latent = jnp.concatenate(latent, axis=1) / row_total

    high = latent.astype(BF16).astype(F32)
    rest = latent - high
    middle = rest.astype(BF16).astype(F32)
    parts = jnp.concatenate([high, middle, rest - middle], axis=0).astype(BF16)
    value = mm(parts, value_up)
    low_value = mm(parts, value_down)
    value = value[0:8] + value[8:16] + value[16:24]
    low_value = low_value[0:8] + low_value[8:16] + low_value[16:24]
    low_value = (low_value * mask).astype(BF16)
    avu_l.wait()
    att[core * CHIPS + chip] = (value + mm(low_value, avu_v[...])).astype(BF16)

    place = core * CHIPS + chip

    def send_att(k, carry):
        send(att.at[place], att.at[place], 8, (me + k) % CTX, group).start()
        return carry

    lax.fori_loop(1, CTX, send_att, 0)
    wo_l.wait()
    arrived(att.at[pl.ds(0, CTX - 1)], 8)
    rows = att[...].astype(F32)
    rows = jnp.concatenate(
        [rows[4 * h : 4 * h + 4].reshape(ROWS, 128) for h in range(HEADS)], axis=1
    ).astype(BF16)
    mixed = mm_t(rows, wo_v[...])
    mixed = jnp.concatenate([mixed, jnp.zeros((ROWS, 128 - WIDTH), F32)], axis=1)
    for y in range(GROUPS):
        part[y] = jnp.concatenate(
            [mixed[2 * y : 2 * y + 2], mixed[REQ + 2 * y : REQ + 2 * y + 2]], axis=0
        )

    def send_part(k, carry):
        there = (group + k) % GROUPS
        send(part.at[there], part_r.at[group], 9, me, there).start()
        return carry

    lax.fori_loop(1, GROUPS, send_part, 0)
    part_r[group] = part[group]
    arrived(part_r.at[pl.ds(0, GROUPS - 1)], 9)
    done = part_r[0]
    for y in range(1, GROUPS):
        done = done + part_r[y]
    out_ref[...] = done

    keeps_key = jnp.logical_and(me // 4 == head_up, me % 4 == me // 16)

    @pl.when(keeps_key)
    def _():
        sent(kw.at[pl.ds(0, 15)], 0)

    @pl.when(jnp.logical_not(keeps_key))
    def _():
        sent(kw, 0)

    share.wait_send()
    sent(qcol.at[pl.ds(0, 3)], 2)
    sent(vw.at[pl.ds(0, CTX - 1)], 3)
    keeps_pe = jnp.logical_and(core == up_core, chip % 4 == quarter)

    @pl.when(keeps_pe)
    def _():
        sent(pos.at[pl.ds(0, 7)], 4)

    @pl.when(jnp.logical_not(keeps_pe))
    def _():
        sent(pos, 4)

    @pl.when(core == up_core)
    def _():
        sent(lat.at[pl.ds(0, CHIPS - 1)], 5)

    @pl.when(core != up_core)
    def _():
        sent(lat, 5)

    sent(ml_r.at[pl.ds(0, CHIPS - 1)], 6)
    sent(acc_r.at[pl.ds(0, CHIPS - 1)], 7)
    sent(att.at[pl.ds(0, CTX - 1)], 8)
    sent(part_r.at[pl.ds(0, GROUPS - 1)], 9)


def body(
    normed_query_latent,
    fresh_token_latent,
    prefix_latent_cache,
    query_up_weight,
    key_up_weight,
    value_up_weight,
    output_weight,
    adapter_query_down,
    adapter_query_up,
    adapter_key_down,
    adapter_key_up,
    adapter_value_down,
    adapter_value_up,
    request_adapter,
    group_first_request,
    group_request_count,
):
    operands = (
        normed_query_latent.reshape(ROWS, -1),
        fresh_token_latent.reshape(ROWS, -1),
        prefix_latent_cache.T,
        query_up_weight.T,
        jnp.transpose(key_up_weight, (0, 2, 1)),
        value_up_weight,
        output_weight.T,
        jnp.transpose(adapter_query_down, (0, 2, 1)).reshape(128, -1),
        adapter_query_up.reshape(128, COLS),
        adapter_key_down,
        adapter_key_up.reshape(128, -1),
        adapter_value_down,
        adapter_value_up.reshape(128, -1),
    )
    vmem = pltpu.VMEM
    done = pl.pallas_call(
        kernel,
        out_shape=jax.ShapeDtypeStruct((4, 128), F32),
        in_specs=[pl.BlockSpec(memory_space=pltpu.HBM)] * 13
        + [pl.BlockSpec(memory_space=pltpu.SMEM)] * 3,
        out_specs=pl.BlockSpec(memory_space=pltpu.VMEM),
        scratch_shapes=[
            vmem((ROWS, 1536), BF16),
            vmem((ROWS, LAT + ROPE), BF16),
            vmem((2, LAT + ROPE, KEYS), BF16),
            vmem((COLS, 1536), BF16),
            vmem((HEADS, 8, 128), BF16),
            vmem((HEADS, 8, 128), BF16),
            vmem((WIDTH, HEADS * 128), BF16),
            vmem((128, 1536), BF16),
            vmem((128, COLS), BF16),
            vmem((8, 8, 16), BF16),
            vmem((128, 128), BF16),
            vmem((8, 8, 16), BF16),
            vmem((128, 128), BF16),
            vmem((HEADS, 16, 128), BF16),
            vmem((HEADS, 16, 128), BF16),
            vmem((16, 16, 128), BF16),
            vmem((CTX, 16, 128), BF16),
            vmem((4, ROWS, 128), BF16),
            vmem((ROWS, 128), BF16),
            vmem((16, 128), BF16),
            vmem((CHIPS, ROWS, 128), BF16),
            vmem((HALF, 16, 128), BF16),
            vmem((CHIPS, ROWS, 128), BF16),
            vmem((CHIPS, ROWS, 128), BF16),
            vmem((2, 2, 128), F32),
            vmem((CHIPS, 2, 128), F32),
            vmem((128, 128), F32),
            vmem((ROWS, 128), F32),
            vmem((ROWS, 128), F32),
            vmem((CTX, 8, 128), BF16),
            vmem((GROUPS, 4, 128), F32),
            vmem((GROUPS, 4, 128), F32),
            pltpu.SemaphoreType.DMA((13,)),
            pltpu.SemaphoreType.DMA((10,)),
            pltpu.SemaphoreType.DMA((10,)),
        ],
        compiler_params=pltpu.CompilerParams(
            collective_id=0, has_side_effects=True, vmem_limit_bytes=48 * 2**20
        ),
        name="latent_attention",
    )(*operands, request_adapter, group_first_request, group_request_count)
    done = done[:, :WIDTH].reshape(2, 2, WIDTH)
    return jnp.transpose(done, (1, 0, 2)).astype(BF16)


def solution(mesh):
    placed = (
        P(),
        P(),
        P("ctx", None),
        P(None, ("head", "ctx")),
        P("head", None, "ctx"),
        P("head", "ctx", None),
        P("head", "ctx"),
        P(),
        P(None, None, ("head", "ctx")),
        P(None, "ctx", None),
        P(None, None, "head"),
        P(None, "ctx", None),
        P(None, None, "head"),
        P(),
        P(),
        P(),
    )
    return jax.shard_map(
        body, mesh=mesh, in_specs=placed, out_specs=P("head", None, "ctx"), check_vma=False
    )
```

time: 680 us -> 70.7 us (0.10); the launches traced: 668 us -> 70 us
  blocking collectives: 288 us -> 0 us
  local copies, waits for them, and re-layouts: 155 us -> 12 us
  waiting for transfers between devices: 101 us -> 0 us
  other arithmetic: 87.2 us -> 0.01 us
  Pallas kernels: 0 us -> 57.9 us
  matrix products: 19.1 us -> 0 us
  between operations: 14.2 us -> 0.05 us
    all_gather x5 -> x0, blocking collectives: 266 us -> none  [the longest x2 103 us: combined_all(): everything = jax.tree.map(lambda part: lax.all_gather(part, axis), shard)]
    dynamic_slice x189 -> x0, local copies, waits for them, and re-layouts: 132 us -> none  [lap(): return combine(so_far, jax.tree.map(lambda part: part[k], everything))]
    all_gather x3 -> x0, waiting for transfers between devices: 100 us -> none  [the longest x2 100 us: combined_all(): everything = jax.tree.map(lambda part: lax.all_gather(part, axis), shard)]
    add x191 -> x0, other arithmetic: 83.5 us -> none  [the longest x63 46.8 us: combine(): row_total = total_first * factor_first + total_second * factor_second]
    pallas_call x0 -> x1, Pallas kernels: none -> 57.9 us  [body(): pl.pallas_call(kernel, out_shape=jax.ShapeDtypeStruct((4, 128), F32), in_...]
    unnamed x1 -> x0, blocking collectives: 22.7 us -> none
    dot_general x14 -> x0, matrix products: 19.1 us -> none  [the longest x1 3.85 us: body(): jnp.einsum('srhc,jc->srhj', joined_query, prefix_latent_cache, preferred_...]
  transfers between devices with their start and end apart: 3 -> 0, of which waited for: 1 -> 0; matrix products, arithmetic and copies ran while one was open for 6% -> 0% of each run, Pallas kernels for 0% -> 0%
where the time goes in v1:
time: 70.7 us; the launch traced here: 70 us
  Pallas kernels  57.9 us (82%)
  local copies, waits for them, and re-layouts  12 us (17%)
    pallas_call x1, Pallas kernels, body(): pl.pallas_call(kernel, out_shape=jax.ShapeDtypeStruct((4, 128), F32), in_...  57.9 us
    unnamed x32, local copies, waits for them, and re-layouts  11.4 us

profile of v1, /device:TPU:1, one launch (start us, length us, event | category | flops | bytes accessed | tf_op | source)
XLA Modules:
  0.0 70.0 jit_solution(15796526084063286699)
XLA Ops:
  0.0 0.0 copy-start.11
  0.0 0.0 copy-start.13
  0.0 0.0 copy-start.14
  0.0 0.0 copy-start.15
  0.0 0.7 copy-done.11
  0.7 0.0 copy-done.13
  0.7 0.0 copy-done.14
  0.7 0.0 copy-done.15
  0.7 0.0 copy-start
  0.7 1.1 %copy-done = bf16[512,576]{0,1:T(8,128)(2,1)S(1)} copy-done((bf16[512,576]{0,1:T(8,128)(2,1)S(1)}, bf16[512,576]{0,1:T(8,128)(2,1)}, u32[]{:S(2)}) %copy-start) | copy-done | bytes 589848
  1.8 0.0 copy-start.1
  1.8 1.0 %copy-done.1 = bf16[8,16,2048]{2,1,0:T(8,128)(2,1)S(1)} copy-done((bf16[8,16,2048]{2,1,0:T(8,128)(2,1)S(1)}, bf16[8,16,2048]{2,1,0:T(8,128)(2,1)}, u32[]{:S(2)}) %copy-start.1) | copy-done | bytes 524312
  2.8 0.0 copy-start.2
  2.8 1.0 %copy-done.2 = bf16[8,16,2048]{2,1,0:T(8,128)(2,1)S(1)} copy-done((bf16[8,16,2048]{2,1,0:T(8,128)(2,1)S(1)}, bf16[8,16,2048]{2,1,0:T(8,128)(2,1)}, u32[]{:S(2)}) %copy-start.2) | copy-done | bytes 524312
  3.9 0.0 copy-start.3
  3.9 1.0 %copy-done.3 = bf16[2048,112]{0,1:T(8,128)(2,1)S(1)} copy-done((bf16[2048,112]{0,1:T(8,128)(2,1)S(1)}, bf16[2048,112]{0,1:T(8,128)(2,1)}, u32[]{:S(2)}) %copy-start.3) | copy-done | bytes 458776
  4.9 0.0 copy-start.4
  4.9 1.0 %copy-done.4 = bf16[8,1536,16]{1,2,0:T(8,128)(2,1)S(1)} copy-done((bf16[8,1536,16]{1,2,0:T(8,128)(2,1)S(1)}, bf16[8,1536,16]{1,2,0:T(8,128)(2,1)}, u32[]{:S(2)}) %copy-start.4) | copy-done | bytes 393240
  5.9 0.0 copy-start.5
  5.9 0.9 %copy-done.5 = bf16[1536,48]{0,1:T(8,128)(2,1)S(1)} copy-done((bf16[1536,48]{0,1:T(8,128)(2,1)S(1)}, bf16[1536,48]{0,1:T(8,128)(2,1)}, u32[]{:S(2)}) %copy-start.5) | copy-done | bytes 147480
  6.8 0.0 copy-start.6
  6.8 0.9 %copy-done.6 = bf16[2,16,1536]{2,1,0:T(8,128)(2,1)S(1)} copy-done((bf16[2,16,1536]{2,1,0:T(8,128)(2,1)S(1)}, bf16[2,16,1536]{2,1,0:T(8,128)(2,1)}, u32[]{:S(2)}) %copy-start.6) | copy-done | bytes 98328
  7.7 0.0 copy-start.7
  7.7 0.8 %copy-done.7 = bf16[2,16,576]{2,1,0:T(8,128)(2,1)S(1)} copy-done((bf16[2,16,576]{2,1,0:T(8,128)(2,1)S(1)}, bf16[2,16,576]{2,1,0:T(8,128)(2,1)}, u32[]{:S(2)}) %copy-start.7) | copy-done | bytes 36888
  8.5 0.0 copy-start.8
  8.5 0.8 %copy-done.8 = bf16[16,128,8]{1,2,0:T(8,128)(2,1)S(1)} copy-done((bf16[16,128,8]{1,2,0:T(8,128)(2,1)S(1)}, bf16[16,128,8]{1,2,0:T(8,128)(2,1)}, u32[]{:S(2)}) %copy-start.8) | copy-done | bytes 32792
  9.2 0.0 copy-start.9
  9.2 0.8 %copy-done.9 = bf16[16,8,128]{2,1,0:T(8,128)(2,1)S(1)} copy-done((bf16[16,8,128]{2,1,0:T(8,128)(2,1)S(1)}, bf16[16,8,128]{2,1,0:T(8,128)(2,1)}, u32[]{:S(2)}) %copy-start.9) | copy-done | bytes 32792
  10.0 0.0 copy-start.10
  10.0 0.8 %copy-done.10 = bf16[8,16,48]{2,1,0:T(8,128)(2,1)S(1)} copy-done((bf16[8,16,48]{2,1,0:T(8,128)(2,1)S(1)}, bf16[8,16,48]{2,1,0:T(8,128)(2,1)}, u32[]{:S(2)}) %copy-start.10) | copy-done | bytes 12312
  10.8 0.0 copy-start.12
  10.8 0.7 %copy-done.12 = bf16[8,8,16]{2,1,0:T(8,128)(2,1)S(1)} copy-done((bf16[8,8,16]{2,1,0:T(8,128)(2,1)S(1)}, bf16[8,8,16]{2,1,0:T(8,128)(2,1)}, u32[]{:S(2)}) %copy-start.12) | copy-done | bytes 2072
  11.5 57.9 %latent_attention.1 = f32[4,128]{1,0:T(4,128)S(1)} custom-call(bf16[32,1536]{1,0:T(8,128)(2,1)S(1)} %bitcast.23, bf16[32,576]{1,0:T(8,128)(2,1)S(1)} %bitcast.24, bf16[576,512]{1,0:T(8,128)(2,1)S(1)} %bitcast.17, bf16[48,1536]{1,0:T(8,128)(2,1)S(1)} %bitcast.22, bf16[16,8,128]{2,1,0:T(8,128)(2,1)S(1)} %bitcast.25, bf16[16,8,128]{2,1,0:T(8,128)(2,1)S(1)} %copy-done.9, ...), custom_call_target="tpu_custom_call" | custom-call | tf_op jit(solution)/shard_map/latent_attention/pallas_call | solution.py:522
  69.4 0.6 copy.19
  (1 shorter events, 0.0 us)
Async XLA Ops:
  0.0 0.7 %copy-start.11 = (bf16[8,8,16]{2,1,0:T(8,128)(2,1)S(1)}, bf16[8,8,16]{2,1,0:T(8,128)(2,1)}, u32[]{:S(2)}) copy-start(bf16[8,8,16]{2,1,0:T(8,128)(2,1)} %akd_hbm.1) | copy-start | bytes 6148
  0.0 0.7 %copy-start.13 = (s32[16]{0:T(128)S(1)}, s32[16]{0:T(128)}, u32[]{:S(2)}) copy-start(s32[16]{0:T(128)} %adapter_s.1) | copy-start | bytes 196
  0.0 0.7 %copy-start.14 = (s32[8]{0:T(128)S(1)}, s32[8]{0:T(128)}, u32[]{:S(2)}) copy-start(s32[8]{0:T(128)} %first_s.1) | copy-start | bytes 100
  0.0 0.7 %copy-start.15 = (s32[8]{0:T(128)S(1)}, s32[8]{0:T(128)}, u32[]{:S(2)}) copy-start(s32[8]{0:T(128)} %count_s.1) | copy-start | bytes 100
  0.7 1.1 %copy-start = (bf16[512,576]{0,1:T(8,128)(2,1)S(1)}, bf16[512,576]{0,1:T(8,128)(2,1)}, u32[]{:S(2)}) copy-start(bf16[512,576]{0,1:T(8,128)(2,1)} %param.18) | copy-start | bytes 1769476
  1.8 1.0 %copy-start.1 = (bf16[8,16,2048]{2,1,0:T(8,128)(2,1)S(1)}, bf16[8,16,2048]{2,1,0:T(8,128)(2,1)}, u32[]{:S(2)}) copy-start(bf16[8,16,2048]{2,1,0:T(8,128)(2,1)} %param.26) | copy-start | bytes 1572868
  2.8 1.0 %copy-start.2 = (bf16[8,16,2048]{2,1,0:T(8,128)(2,1)S(1)}, bf16[8,16,2048]{2,1,0:T(8,128)(2,1)}, u32[]{:S(2)}) copy-start(bf16[8,16,2048]{2,1,0:T(8,128)(2,1)} %param.28) | copy-start | bytes 1572868
  3.9 1.0 %copy-start.3 = (bf16[2048,112]{0,1:T(8,128)(2,1)S(1)}, bf16[2048,112]{0,1:T(8,128)(2,1)}, u32[]{:S(2)}) copy-start(bf16[2048,112]{0,1:T(8,128)(2,1)} %param.22) | copy-start | bytes 1376260
  4.9 1.0 %copy-start.4 = (bf16[8,1536,16]{1,2,0:T(8,128)(2,1)S(1)}, bf16[8,1536,16]{1,2,0:T(8,128)(2,1)}, u32[]{:S(2)}) copy-start(bf16[8,1536,16]{1,2,0:T(8,128)(2,1)} %param.23) | copy-start | bytes 1179652
  5.9 0.9 %copy-start.5 = (bf16[1536,48]{0,1:T(8,128)(2,1)S(1)}, bf16[1536,48]{0,1:T(8,128)(2,1)}, u32[]{:S(2)}) copy-start(bf16[1536,48]{0,1:T(8,128)(2,1)} %param.19) | copy-start | bytes 442372
  6.8 0.9 %copy-start.6 = (bf16[2,16,1536]{2,1,0:T(8,128)(2,1)S(1)}, bf16[2,16,1536]{2,1,0:T(8,128)(2,1)}, u32[]{:S(2)}) copy-start(bf16[2,16,1536]{2,1,0:T(8,128)(2,1)} %param.16) | copy-start | bytes 294916
  7.7 0.8 %copy-start.7 = (bf16[2,16,576]{2,1,0:T(8,128)(2,1)S(1)}, bf16[2,16,576]{2,1,0:T(8,128)(2,1)}, u32[]{:S(2)}) copy-start(bf16[2,16,576]{2,1,0:T(8,128)(2,1)} %param.17) | copy-start | bytes 110596
  8.5 0.8 %copy-start.8 = (bf16[16,128,8]{1,2,0:T(8,128)(2,1)S(1)}, bf16[16,128,8]{1,2,0:T(8,128)(2,1)}, u32[]{:S(2)}) copy-start(bf16[16,128,8]{1,2,0:T(8,128)(2,1)} %param.20) | copy-start | bytes 98308
  9.2 0.8 %copy-start.9 = (bf16[16,8,128]{2,1,0:T(8,128)(2,1)S(1)}, bf16[16,8,128]{2,1,0:T(8,128)(2,1)}, u32[]{:S(2)}) copy-start(bf16[16,8,128]{2,1,0:T(8,128)(2,1)} %vup_hbm.1) | copy-start | bytes 98308
  10.0 0.8 %copy-start.10 = (bf16[8,16,48]{2,1,0:T(8,128)(2,1)S(1)}, bf16[8,16,48]{2,1,0:T(8,128)(2,1)}, u32[]{:S(2)}) copy-start(bf16[8,16,48]{2,1,0:T(8,128)(2,1)} %param.24) | copy-start | bytes 36868
  10.8 0.7 %copy-start.12 = (bf16[8,8,16]{2,1,0:T(8,128)(2,1)S(1)}, bf16[8,8,16]{2,1,0:T(8,128)(2,1)}, u32[]{:S(2)}) copy-start(bf16[8,8,16]{2,1,0:T(8,128)(2,1)} %avd_hbm.1) | copy-start | bytes 6148

commit v2 on v1

v2 whole, which is shorter than its diff:
```python
import functools
import math

import jax
import jax.numpy as jnp
from jax import lax
from jax.experimental import pallas as pl
from jax.experimental.pallas import tpu as pltpu
from jax.sharding import PartitionSpec as P

MESH = pl.DeviceIdType.MESH
F32 = jnp.float32
BF16 = jnp.bfloat16

CTX = 64
CHIPS = CTX // 2
GROUPS = 8
HEADS = 16
HALF = HEADS // 2
ROWS = 32
REQ = 16
NOPE = 128
ROPE = 64
LAT = 512
COLS = 48
KEYS = 512
WIDTH = 112
SCALE = 1.0 / math.sqrt(NOPE + ROPE)


def mm(a, b):
    return lax.dot_general(a, b, (((1,), (0,)), ((), ())), preferred_element_type=F32)


def mm_t(a, b):
    return lax.dot_general(a, b, (((1,), (1,)), ((), ())), preferred_element_type=F32)


def far_first(i, size):
    return size // 2 + ((i + 1) >> 1) * (1 - 2 * (i & 1))


def kernel(
    x_hbm,
    fresh_hbm,
    cache_hbm,
    wq_hbm,
    kup_hbm,
    vup_hbm,
    wo_hbm,
    aqd_hbm,
    aqu_hbm,
    akd_hbm,
    aku_hbm,
    avd_hbm,
    avu_hbm,
    adapter_s,
    first_s,
    count_s,
    out_ref,
    x_v,
    fresh_v,
    cache_v,
    wq_v,
    kup_v,
    vup_v,
    wo_v,
    aqd_v,
    aqu_v,
    akd_v,
    aku_v,
    avd_v,
    avu_v,
    kmsg,
    vmsg,
    kw,
    vw,
    col_s,
    qcol,
    lq_s,
    pe_s,
    lat,
    pos,
    acc_s,
    acc_r,
    ml_s,
    ml_r,
    turned,
    att,
    part,
    part_r,
    ready,
    load_sem,
    send_sem,
    recv_sem,
):
    me = lax.axis_index("ctx")
    group = lax.axis_index("head")
    chip = me >> 1
    core = me & 1
    x_at = me >> 4
    z_at = chip & 7
    place = me & 15
    head_made = me >> 2
    piece = me & 3
    head_up = 4 * (place & 3) + (place >> 2)
    up_core = head_up >> 3
    head_own = (chip ^ 4) >> 1
    block_own = (chip & 15) ^ 4
    step_own = chip & 1
    owner = core == chip >> 4

    def chip_at(i):
        dz = far_first(i >> 2, 8)
        dx = far_first(i & 3, 4)
        return (((x_at + dx) & 3) << 3) | ((z_at + dz) & 7)

    def group_of(z_there, pair):
        step = (pair - (z_there >> 1)) & 3
        near = jnp.logical_or(step == 0, step == 3 - 2 * (z_there & 1))
        return jnp.where(near, 0, 1)

    barrier = pltpu.get_barrier_semaphore()

    def greet(ctx, y):
        pl.semaphore_signal(barrier, inc=1, device_id=(ctx, y), device_id_type=MESH)

    def greet_plane(i, carry):
        z = (z_at + far_first(i, 8)) & 7
        greet(16 * x_at + 2 * z + core, group)
        greet(16 * x_at + 2 * z + 1 - core, group)
        return carry

    lax.fori_loop(0, 7, greet_plane, 0)
    line = [16 * ((x_at + d) & 3) + place for d in (2, 1, 3)]
    for ctx in line:
        greet(ctx, group)

    @pl.when(head_up >> 2 != x_at)
    def _():
        for n in range(4):
            greet(4 * head_up + n, group)

    def greet_group(i, carry):
        y = (group + far_first(i, GROUPS)) & (GROUPS - 1)
        greet(me, y)
        greet(me ^ 1, y)
        return carry

    lax.fori_loop(0, GROUPS - 1, greet_group, 0)
    greet(me ^ 1, group)

    up_col = pl.multiple_of(head_up * NOPE, NOPE)
    own_col = pl.multiple_of(head_own * NOPE, NOPE)
    half_col = pl.multiple_of(core * (HALF * NOPE), HALF * NOPE)
    other_col = pl.multiple_of((1 - core) * (HALF * NOPE), HALF * NOPE)
    pending = {}
    for n, (name, src, dst) in enumerate(
        (
            ("x", x_hbm, x_v),
            ("aqd", aqd_hbm, aqd_v),
            ("wq", wq_hbm, wq_v),
            ("aqu", aqu_hbm, aqu_v),
            ("kup", kup_hbm, kup_v),
            ("akd", akd_hbm, akd_v),
            ("vup", vup_hbm, vup_v),
            ("avd", avd_hbm, avd_v),
            ("aku", aku_hbm.at[:, pl.ds(up_col, NOPE)], aku_v),
            ("cache", cache_hbm, cache_v.at[0]),
            ("fresh", fresh_hbm, fresh_v),
            ("avu", avu_hbm.at[:, pl.ds(own_col, NOPE)], avu_v),
            ("wo", wo_hbm.at[:, pl.ds(half_col, HALF * NOPE)], wo_v.at[0]),
        )
    ):
        load = pltpu.make_async_copy(src, dst, load_sem.at[n])
        load.start()
        pending[name] = load.wait

    def wait(*names):
        for name in names:
            pending.pop(name)()

    def finish():
        wait(*list(pending))

    def send(src, dst, n, ctx, y, out=None):
        return pltpu.make_async_remote_copy(
            src_ref=src,
            dst_ref=dst,
            send_sem=send_sem.at[n if out is None else out],
            recv_sem=recv_sem.at[n],
            device_id=(ctx, y),
            device_id_type=MESH,
        )

    def send_or_keep(src, dst, n, ctx, y=None, out=None):
        y = group if y is None else y
        here = jnp.logical_and(ctx == me, y == group)

        @pl.when(here)
        def _():
            pltpu.make_async_copy(src, dst, recv_sem.at[n]).start()

        @pl.when(jnp.logical_not(here))
        def _():
            send(src, dst, n, ctx, y, out).start()

    def arrives(name, ref, n, when=None):
        wait_all = pltpu.make_async_copy(ref, ref, recv_sem.at[n]).wait
        pending[name] = wait_all if when is None else lambda: pl.when(when)(wait_all)

    def leaves(name, ref, n, kept=None, fewer=None):
        wait_all = pltpu.make_async_copy(ref, ref, send_sem.at[n]).wait

        def either():
            pl.when(kept)(pltpu.make_async_copy(fewer, fewer, send_sem.at[n]).wait)
            pl.when(jnp.logical_not(kept))(wait_all)

        pending[name] = wait_all if kept is None else either

    lane_adapter = lax.broadcasted_iota(jnp.int32, (REQ, 128), 1) // 16
    request = lax.broadcasted_iota(jnp.int32, (REQ, 128), 0)
    adapter = jnp.zeros((REQ, 128), jnp.int32)
    first = jnp.zeros((REQ, 128), jnp.int32)
    count = jnp.zeros((REQ, 128), jnp.int32)
    for r in range(REQ):
        adapter = jnp.where(request == r, adapter_s[r], adapter)
    for a in range(8):
        first = jnp.where(lane_adapter == a, first_s[a], first)
        count = jnp.where(lane_adapter == a, count_s[a], count)
    owns = adapter == lane_adapter
    within = request - first
    live = jnp.logical_and(owns, jnp.logical_and(within >= 0, within < count))
    own_mask = jnp.where(owns, 1.0, 0.0).astype(F32)
    live_mask = jnp.where(live, 1.0, 0.0).astype(F32)
    live_mask = jnp.concatenate([live_mask, live_mask], axis=0)

    wait("x", "aqd")
    x = x_v[...]
    low = (mm_t(x, aqd_v[...]) * live_mask).astype(BF16)
    wait("wq", "aqu")
    cols = (mm_t(x, wq_v[...]) + mm(low, aqu_v[...])).astype(BF16)
    col_s[...] = jnp.concatenate(
        [cols.astype(F32), jnp.zeros((ROWS, 128 - COLS), F32)], axis=1
    ).astype(BF16)

    wait("kup", "akd")
    table = jnp.concatenate([akd_v[a].astype(F32) for a in range(8)], axis=1)
    for h in range(HEADS):
        kmsg[h] = jnp.concatenate([kup_v[h].astype(F32), table], axis=0).astype(BF16)
    wait("vup", "avd")
    table = jnp.concatenate([avd_v[a].astype(F32) for a in range(8)], axis=1)
    for h in range(HEADS):
        vmsg[h] = jnp.concatenate([vup_v[h].astype(F32), table], axis=0).astype(BF16)

    pl.semaphore_wait(barrier, 15 + 3 + 3 + 2 * (GROUPS - 1))
    for ctx in line:
        pl.semaphore_signal(ready, inc=1, device_id=(ctx, group), device_id_type=MESH)
    pending["ready"] = lambda: pl.semaphore_wait(ready, 3)

    def send_keys(i, carry):
        z = (z_at + far_first(i, 8)) & 7
        for c in range(2):
            to = 2 * z + c
            send_or_keep(
                kmsg.at[4 * (to & 3) + (to >> 2)], kw.at[place], 0, 16 * x_at + to
            )
        return carry

    lax.fori_loop(0, 8, send_keys, 0)
    arrives("kw", kw, 0)
    leaves("kw out", kw.at[pl.ds(0, 15)], 0)

    to = ((head_made & 3) << 2) | (head_made >> 2)
    for i in range(4):
        send_or_keep(
            col_s, qcol.at[piece], 2, 16 * ((x_at + (2, 1, 3, 0)[i]) & 3) + to
        )
    arrives("qcol", qcol, 2)
    leaves("qcol out", qcol, 2, piece == x_at, qcol.at[pl.ds(0, 3)])

    wait("qcol")
    q0 = qcol[0].astype(F32)
    q1 = qcol[1].astype(F32)
    q2 = qcol[2].astype(F32)
    q3 = qcol[3].astype(F32)
    nope = jnp.concatenate([q0[:, :48], q1[:, :48], q2[:, :32]], axis=1).astype(BF16)
    pe = jnp.concatenate([q2[:, 32:48], q3[:, :48]], axis=1)
    pe_s[...] = jnp.concatenate([pe[:16], pe[16:]], axis=1).astype(BF16)

    wait("ready")

    def send_pe(i, carry):
        z = (z_at + far_first(i, 8)) & 7
        n = 4 + 8 * group_of(z, z_at >> 1)
        send_or_keep(
            pe_s, pos.at[head_up & 7], n, 16 * x_at + 2 * z + up_core, out=4
        )
        return carry

    lax.fori_loop(0, 8, send_pe, 0)
    half_pos = pos.at[pl.ds(0, HALF // 2)]
    arrives("pos 0", half_pos, 4)
    arrives("pos 1", half_pos, 12)
    leaves("pos out", pos, 4, core == up_core, pos.at[pl.ds(0, 7)])

    wait("aku")
    low_key = (mm_t(nope, aku_v[...]) * live_mask).astype(BF16)
    wait("kw")
    kwf = kw[...].astype(F32)
    key_up = kwf[:, :8].reshape(128, 128).astype(BF16)
    key_down = kwf[:, 8:].reshape(128, 128).astype(BF16)
    lq_s[...] = (mm_t(nope, key_up) + mm_t(low_key, key_down)).astype(BF16)

    slot = (head_up & 7) * 4 + x_at

    def send_lat(i, carry):
        there = chip_at(i)
        n = 5 + 6 * group_of(there & 7, z_at >> 1)
        send_or_keep(lq_s, lat.at[slot], n, 2 * there + up_core, out=5)
        return carry

    lax.fori_loop(0, CHIPS, send_lat, 0)
    leaves("lat out", lat, 5, core == up_core, lat.at[pl.ds(0, CHIPS - 1)])
    half_lat = lat.at[pl.ds(0, CHIPS // 2)]
    arrives("lat 0", half_lat, 5)
    arrives("lat 1", half_lat, 11)

    share = send(cache_hbm, cache_v.at[1], 1, me ^ 1, group)
    share.start()
    pending["share"] = share.wait_recv
    pending["share out"] = share.wait_send
    share = send(
        wo_hbm.at[:, pl.ds(other_col, HALF * NOPE)], wo_v.at[1], 10, me ^ 1, group
    )
    share.start()
    pending["wo share"] = share.wait_recv
    pending["wo share out"] = share.wait_send

    def send_values(i, carry):
        there = chip_at(i)
        send_or_keep(vmsg.at[(there ^ 4) >> 1], vw.at[me], 3, 2 * there + (there >> 4))
        return carry

    lax.fori_loop(0, CHIPS, send_values, 0)
    arrives("vw", vw, 3, owner)
    leaves(
        "vw out", vw.at[pl.ds(0, CHIPS)], 3, owner, vw.at[pl.ds(0, CHIPS - 1)]
    )

    next_pair = 2 * (z_at & 1) - 1
    pairs = [((z_at >> 1) + d) & 3 for d in (0, next_pair, 2, -next_pair)]

    def owner_of(block):
        return 2 * (16 * core + (block ^ 4)) + core

    for half in range(2):
        heads = [pairs[2 * half + (n >> 1)] + 4 * (n & 1) for n in range(4)]
        wait("pos %d" % half, "lat %d" % half)
        q_lat = jnp.concatenate(
            [
                jnp.concatenate([lat[4 * h + j] for j in range(4)], axis=1)
                for h in heads
            ],
            axis=0,
        )
        q_pe = []
        for h in heads:
            both = pos[h].astype(F32)
            q_pe += [both[:, :ROPE], both[:, ROPE:]]
        q_pe = jnp.concatenate(q_pe, axis=0).astype(BF16)
        if half == 0:
            wait("cache", "share")
        scores = [
            (mm(q_lat, cache_v[n, :LAT]) + mm(q_pe, cache_v[n, LAT:])) * SCALE
            for n in range(2)
        ]
        top = jnp.maximum(
            jnp.max(scores[0], axis=1, keepdims=True),
            jnp.max(scores[1], axis=1, keepdims=True),
        )
        weights = [jnp.exp(s - top) for s in scores]
        total = jnp.sum(weights[0], axis=1, keepdims=True) + jnp.sum(
            weights[1], axis=1, keepdims=True
        )
        lane = lax.broadcasted_iota(jnp.int32, (128, 128), 1)
        stats = jnp.where(lane == 0, top, jnp.where(lane == 1, total, 0.0)).T[:2]
        for n, h in enumerate(heads):
            ml_s[h] = stats if n == 0 else pltpu.roll(stats, 128 - 32 * n, 1)

        for h in heads:
            for step in range(2):
                send_or_keep(ml_s.at[h], ml_r.at[chip], 6, owner_of(2 * h + step))

        summed = sum(mm_t(weights[n].astype(BF16), cache_v[n, :LAT]) for n in range(2))
        for n, h in enumerate(heads):
            for step in range(2):
                rows = summed[32 * n + 16 * step : 32 * n + 16 * step + 16]
                for j in range(4):
                    acc_s[2 * h + step, 16 * j : 16 * j + 16] = rows[
                        :, 128 * j : 128 * j + 128
                    ].astype(BF16)

        for h in heads:
            for step in range(2):
                block = 2 * h + step
                send_or_keep(acc_s.at[block], acc_r.at[chip], 7, owner_of(block))

    arrives("ml", ml_r, 6, owner)
    leaves("ml out", ml_r.at[pl.ds(0, 16)], 6, owner, ml_r.at[pl.ds(0, 15)])
    arrives("acc", acc_r, 7, owner)
    leaves("acc out", acc_r.at[pl.ds(0, 16)], 7, owner, acc_r.at[pl.ds(0, 15)])

    wait("fresh", "avu")
    for name in ("vw", "ml", "acc"):
        pending.pop(name)

    def arrived(ref, n):
        pltpu.make_async_copy(ref, ref, recv_sem.at[n]).wait()

    @pl.when(owner)
    def _():
        fresh = fresh_v[...]
        own = head_own & 7
        own_rows = pl.ds(pl.multiple_of(REQ * step_own, REQ), REQ)
        own_lat = jnp.concatenate([lat[4 * own + j, own_rows] for j in range(4)], axis=1)
        both = pos[own].astype(F32)
        own_pe = jnp.where(step_own == 0, both[:, :ROPE], both[:, ROPE:]).astype(BF16)
        own_scores = (
            mm_t(own_lat, fresh[:, :LAT]) + mm_t(own_pe, fresh[:, LAT:])
        ) * SCALE
        row = lax.broadcasted_iota(jnp.int32, (REQ, ROWS), 0)
        key = lax.broadcasted_iota(jnp.int32, (REQ, ROWS), 1)
        seen = jnp.logical_and(row == key % REQ, key // REQ <= step_own)
        own_scores = jnp.where(seen, own_scores, -jnp.inf)
        own_top = jnp.max(own_scores, axis=1, keepdims=True)
        own_weights = jnp.exp(own_scores - own_top)
        own_total = jnp.sum(own_weights, axis=1, keepdims=True)
        own_sum = mm(own_weights.astype(BF16), fresh[:, :LAT])

        arrived(vw, 3)
        vwf = vw[...].astype(F32)
        value_up = vwf[:, :8].reshape(LAT, 128).astype(BF16)
        value_down = vwf[:, 8:].reshape(LAT, 128).astype(BF16)

        arrived(ml_r, 6)
        ml = ml_r[...]
        turned[...] = jnp.concatenate(
            [ml[:, 0], ml[:, 1], jnp.zeros((64, 128), F32)], axis=0
        ).T
        stats = turned[pl.ds(pl.multiple_of(REQ * step_own, REQ), REQ), :]
        tops = stats[:, :CHIPS]
        totals = stats[:, CHIPS : 2 * CHIPS]
        joined = jnp.maximum(jnp.max(tops, axis=1, keepdims=True), own_top)
        factors = jnp.exp(tops - joined)
        own_factor = jnp.exp(own_top - joined)
        row_total = (
            jnp.sum(factors * totals, axis=1, keepdims=True) + own_factor * own_total
        )
        latent = own_sum * own_factor
        latent = [latent[:, 128 * j : 128 * j + 128] for j in range(4)]
        arrived(acc_r, 7)
        for n in range(CHIPS):
            factor = factors[:, n : n + 1]
            for j in range(4):
                got = acc_r[n, REQ * j : REQ * j + REQ].astype(F32)
                latent[j] = latent[j] + factor * got
        latent = jnp.concatenate(latent, axis=1) / row_total

        high = latent.astype(BF16)
        rest = latent - high.astype(F32)
        middle = rest.astype(BF16)
        low = (rest - middle.astype(F32)).astype(BF16)
        parts = jnp.concatenate([high, middle, low], axis=0)
        value = mm(parts, value_up)
        low_value = mm(parts, value_down)
        value = value[:16] + value[16:32] + value[32:48]
        low_value = low_value[:16] + low_value[16:32] + low_value[32:48]
        low_value = (low_value * own_mask).astype(BF16)
        att[block_own] = (value + mm(low_value, avu_v[...])).astype(BF16)


    @pl.when(owner)
    def _():
        def send_att(i, carry):
            send(
                att.at[block_own], att.at[block_own], 8, 2 * chip_at(i) + core, group
            ).start()
            return carry

        lax.fori_loop(0, CHIPS - 1, send_att, 0)

    wait("wo", "wo share")
    all_here = pltpu.make_async_copy(att, att, recv_sem.at[8]).wait
    but_own = att.at[pl.ds(0, 15)]
    pl.when(owner)(pltpu.make_async_copy(but_own, but_own, recv_sem.at[8]).wait)
    pl.when(jnp.logical_not(owner))(all_here)
    many = acc_r.at[0, pl.ds(0, 16)]

    def all_sent():
        def one(i, carry):
            pltpu.make_async_copy(many, many, send_sem.at[8]).wait()
            return carry

        lax.fori_loop(0, CHIPS - 1, one, 0)

    pending["att out"] = lambda: pl.when(owner)(all_sent)
    rows = jnp.concatenate(
        [
            jnp.concatenate([att[2 * h], att[2 * h + 1]], axis=0)
            for h in range(HALF)
        ],
        axis=1,
    )
    for n in range(2):
        mixed = mm_t(rows, wo_v[n])
        mixed = jnp.concatenate([mixed, jnp.zeros((ROWS, 128 - WIDTH), F32)], axis=1)
        for y in range(GROUPS):
            part[n, y] = jnp.concatenate(
                [mixed[2 * y : 2 * y + 2], mixed[REQ + 2 * y : REQ + 2 * y + 2]], axis=0
            )

    def send_part(i, carry):
        y = (group + far_first(i, GROUPS)) & (GROUPS - 1)
        for n in range(2):
            send_or_keep(
                part.at[n, y], part_r.at[2 * group + core], 9, me ^ n, y
            )
        return carry

    lax.fori_loop(0, GROUPS, send_part, 0)
    arrives("part", part_r, 9)
    leaves("part out", part_r.at[pl.ds(0, 2 * GROUPS - 1)], 9)
    wait("part")
    done = part_r[0]
    for n in range(1, 2 * GROUPS):
        done = done + part_r[n]
    done = done[:, :WIDTH].astype(BF16)
    for step in range(2):
        for r in range(2):
            out_ref[r, step : step + 1, :] = done[2 * step + r : 2 * step + r + 1]

    finish()


def body(
    normed_query_latent,
    fresh_token_latent,
    prefix_latent_cache,
    query_up_weight,
    key_up_weight,
    value_up_weight,
    output_weight,
    adapter_query_down,
    adapter_query_up,
    adapter_key_down,
    adapter_key_up,
    adapter_value_down,
    adapter_value_up,
    request_adapter,
    group_first_request,
    group_request_count,
):
    operands = (
        normed_query_latent.reshape(ROWS, -1),
        fresh_token_latent.reshape(ROWS, -1),
        prefix_latent_cache.T,
        query_up_weight.T,
        jnp.transpose(key_up_weight, (0, 2, 1)),
        value_up_weight,
        output_weight.T,
        jnp.transpose(adapter_query_down, (0, 2, 1)).reshape(128, -1),
        adapter_query_up.reshape(128, COLS),
        adapter_key_down,
        adapter_key_up.reshape(128, -1),
        adapter_value_down,
        adapter_value_up.reshape(128, -1),
    )
    vmem = pltpu.VMEM
    return pl.pallas_call(
        kernel,
        out_shape=jax.ShapeDtypeStruct((2, 2, WIDTH), BF16),
        in_specs=[pl.BlockSpec(memory_space=pl.ANY)] * 13
        + [pl.BlockSpec(memory_space=pltpu.SMEM)] * 3,
        out_specs=pl.BlockSpec(memory_space=pltpu.VMEM),
        scratch_shapes=[
            vmem((ROWS, 1536), BF16),
            vmem((ROWS, LAT + ROPE), BF16),
            vmem((2, LAT + ROPE, KEYS), BF16),
            vmem((COLS, 1536), BF16),
            vmem((HEADS, 8, 128), BF16),
            vmem((HEADS, 8, 128), BF16),
            vmem((2, WIDTH, HALF * 128), BF16),
            vmem((128, 1536), BF16),
            vmem((128, COLS), BF16),
            vmem((8, 8, 16), BF16),
            vmem((128, 128), BF16),
            vmem((8, 8, 16), BF16),
            vmem((128, 128), BF16),
            vmem((HEADS, 16, 128), BF16),
            vmem((HEADS, 16, 128), BF16),
            vmem((16, 16, 128), BF16),
            vmem((CTX, 16, 128), BF16),
            vmem((ROWS, 128), BF16),
            vmem((4, ROWS, 128), BF16),
            vmem((ROWS, 128), BF16),
            vmem((16, 128), BF16),
            vmem((CHIPS, ROWS, 128), BF16),
            vmem((HALF, 16, 128), BF16),
            vmem((16, 4 * REQ, 128), BF16),
            vmem((CHIPS, 4 * REQ, 128), BF16),
            vmem((HALF, 2, 128), F32),
            vmem((CHIPS, 2, 128), F32),
            vmem((128, 128), F32),
            vmem((16, 16, 128), BF16),
            vmem((2, GROUPS, 4, 128), F32),
            vmem((2 * GROUPS, 4, 128), F32),
            pltpu.SemaphoreType.REGULAR,
            pltpu.SemaphoreType.DMA((13,)),
            pltpu.SemaphoreType.DMA((11,)),
            pltpu.SemaphoreType.DMA((13,)),
        ],
        compiler_params=pltpu.CompilerParams(
            collective_id=0, has_side_effects=True, vmem_limit_bytes=60 * 2**20
        ),
        name="latent_attention",
    )(*operands, request_adapter, group_first_request, group_request_count)


def solution(mesh):
    placed = (
        P(),
        P(),
        P("ctx", None),
        P(None, ("head", "ctx")),
        P("head", None, "ctx"),
        P("head", "ctx", None),
        P("head", "ctx"),
        P(),
        P(None, None, ("head", "ctx")),
        P(None, "ctx", None),
        P(None, None, "head"),
        P(None, "ctx", None),
        P(None, None, "head"),
        P(),
        P(),
        P(),
    )
    return jax.shard_map(
        body, mesh=mesh, in_specs=placed, out_specs=P("head", None, "ctx"), check_vma=False
    )
```

time: 70.7 us -> 53.7 us (0.76)
  local copies, waits for them, and re-layouts: 12 us -> 1.25 us
  Pallas kernels: 57.9 us -> 52.3 us
    unnamed x32 -> x1, local copies, waits for them, and re-layouts: 11.4 us -> 1.25 us
    pallas_call x1, Pallas kernels: 57.9 us -> 52.3 us  [body(): pl.pallas_call(kernel, out_shape=jax.ShapeDtypeStruct((2, 2, WIDTH), BF16...]
where the time goes in v2:
time: 53.7 us; the launch traced here: 53.5 us
  Pallas kernels  52.3 us (97%)
  local copies, waits for them, and re-layouts  1.25 us (2%)
    pallas_call x1, Pallas kernels, body(): pl.pallas_call(kernel, out_shape=jax.ShapeDtypeStruct((2, 2, WIDTH), BF16...  52.3 us
    unnamed x1, local copies, waits for them, and re-layouts  1.25 us

profile of v2, /device:TPU:1, one launch (start us, length us, event | category | flops | bytes accessed | tf_op | source)
XLA Modules:
  0.0 53.5 jit_solution(9092420096985895538)
XLA Ops:
  0.0 52.3 %latent_attention.1 = bf16[2,2,112]{2,1,0:T(2,128)(2,1)} custom-call(bf16[32,1536]{1,0:T(8,128)(2,1)} %bitcast.18, bf16[32,576]{1,0:T(8,128)(2,1)} %bitcast.19, bf16[576,512]{1,0:T(8,128)(2,1)} %bitcast.12, bf16[48,1536]{1,0:T(8,128)(2,1)} %bitcast.17, bf16[16,8,128]{2,1,0:T(8,128)(2,1)} %bitcast.20, bf16[16,8,128]{2,1,0:T(8,128)(2,1)} %vup_hbm.1, ...), custom_call_target="tpu_custom_call" | custom-call | tf_op jit(solution)/shard_map/latent_attention/pallas_call | solution.py:580
  52.3 1.2 %copy.18 = bf16[2,2,112]{2,1,0:T(2,128)(2,1)} copy(bf16[2,2,112]{2,1,0:T(2,128)(2,1)} %latent_attention.1) | data formatting | bytes 1792

commit v3 on v2

--- a/solution.py
+++ b/solution.py
@@ -25,6 +25,7 @@
 COLS = 48
 KEYS = 512
 WIDTH = 112
+PAIRS = 4
 SCALE = 1.0 / math.sqrt(NOPE + ROPE)
 
 
@@ -117,8 +118,9 @@
 
     def group_of(z_there, pair):
         step = (pair - (z_there >> 1)) & 3
-        near = jnp.logical_or(step == 0, step == 3 - 2 * (z_there & 1))
-        return jnp.where(near, 0, 1)
+        nearer = 3 - 2 * (z_there & 1)
+        beside = jnp.where(step == nearer, 1, 2)
+        return jnp.where(step == 0, 0, jnp.where(step == 2, 3, beside))
 
     barrier = pltpu.get_barrier_semaphore()
 
@@ -248,10 +250,6 @@
     table = jnp.concatenate([akd_v[a].astype(F32) for a in range(8)], axis=1)
     for h in range(HEADS):
         kmsg[h] = jnp.concatenate([kup_v[h].astype(F32), table], axis=0).astype(BF16)
-    wait("vup", "avd")
-    table = jnp.concatenate([avd_v[a].astype(F32) for a in range(8)], axis=1)
-    for h in range(HEADS):
-        vmsg[h] = jnp.concatenate([vup_v[h].astype(F32), table], axis=0).astype(BF16)
 
     pl.semaphore_wait(barrier, 15 + 3 + 3 + 2 * (GROUPS - 1))
     for ctx in line:
@@ -262,12 +260,15 @@
         z = (z_at + far_first(i, 8)) & 7
         for c in range(2):
             to = 2 * z + c
-            send_or_keep(
-                kmsg.at[4 * (to & 3) + (to >> 2)], kw.at[place], 0, 16 * x_at + to
-            )
+            src = kmsg.at[4 * (to & 3) + (to >> 2)]
+            send(src, kw.at[place], 0, 16 * x_at + to, group).start()
         return carry
 
-    lax.fori_loop(0, 8, send_keys, 0)
+    lax.fori_loop(0, 7, send_keys, 0)
+    to = place ^ 1
+    src = kmsg.at[4 * (to & 3) + (to >> 2)]
+    send(src, kw.at[place], 0, me ^ 1, group).start()
+    pltpu.make_async_copy(kmsg.at[head_up], kw.at[place], recv_sem.at[0]).start()
     arrives("kw", kw, 0)
     leaves("kw out", kw.at[pl.ds(0, 15)], 0)
 
@@ -292,16 +293,15 @@
 
     def send_pe(i, carry):
         z = (z_at + far_first(i, 8)) & 7
-        n = 4 + 8 * group_of(z, z_at >> 1)
+        n = 12 + 2 * group_of(z, z_at >> 1)
         send_or_keep(
             pe_s, pos.at[head_up & 7], n, 16 * x_at + 2 * z + up_core, out=4
         )
         return carry
 
     lax.fori_loop(0, 8, send_pe, 0)
-    half_pos = pos.at[pl.ds(0, HALF // 2)]
-    arrives("pos 0", half_pos, 4)
-    arrives("pos 1", half_pos, 12)
+    for n in range(PAIRS):
+        arrives("pos %d" % n, pos.at[pl.ds(0, HALF // PAIRS)], 12 + 2 * n)
     leaves("pos out", pos, 4, core == up_core, pos.at[pl.ds(0, 7)])
 
     wait("aku")
@@ -316,15 +316,15 @@
 
     def send_lat(i, carry):
         there = chip_at(i)
-        n = 5 + 6 * group_of(there & 7, z_at >> 1)
-        send_or_keep(lq_s, lat.at[slot], n, 2 * there + up_core, out=5)
+        n = 11 + 2 * group_of(there & 7, z_at >> 1)
+        send(lq_s, lat.at[slot], n, 2 * there + up_core, group, out=5).start()
         return carry
 
-    lax.fori_loop(0, CHIPS, send_lat, 0)
+    lax.fori_loop(0, CHIPS - 1, send_lat, 0)
+    send_or_keep(lq_s, lat.at[slot], 11, 2 * chip + up_core, out=5)
     leaves("lat out", lat, 5, core == up_core, lat.at[pl.ds(0, CHIPS - 1)])
-    half_lat = lat.at[pl.ds(0, CHIPS // 2)]
-    arrives("lat 0", half_lat, 5)
-    arrives("lat 1", half_lat, 11)
+    for n in range(PAIRS):
+        arrives("lat %d" % n, lat.at[pl.ds(0, CHIPS // PAIRS)], 11 + 2 * n)
 
     share = send(cache_hbm, cache_v.at[1], 1, me ^ 1, group)
     share.start()
@@ -337,26 +337,34 @@
     pending["wo share"] = share.wait_recv
     pending["wo share out"] = share.wait_send
 
+    wait("vup", "avd")
+    table = jnp.concatenate([avd_v[a].astype(F32) for a in range(8)], axis=1)
+    for h in range(HEADS):
+        vmsg[h] = jnp.concatenate([vup_v[h].astype(F32), table], axis=0).astype(BF16)
+
     def send_values(i, carry):
         there = chip_at(i)
-        send_or_keep(vmsg.at[(there ^ 4) >> 1], vw.at[me], 3, 2 * there + (there >> 4))
+        send(
+            vmsg.at[(there ^ 4) >> 1], vw.at[me], 3, 2 * there + (there >> 4), group
+        ).start()
         return carry
 
-    lax.fori_loop(0, CHIPS, send_values, 0)
+    lax.fori_loop(0, CHIPS - 1, send_values, 0)
+    send_or_keep(vmsg.at[head_own], vw.at[me], 3, 2 * chip + (chip >> 4))
     arrives("vw", vw, 3, owner)
     leaves(
         "vw out", vw.at[pl.ds(0, CHIPS)], 3, owner, vw.at[pl.ds(0, CHIPS - 1)]
     )
 
     next_pair = 2 * (z_at & 1) - 1
-    pairs = [((z_at >> 1) + d) & 3 for d in (0, next_pair, 2, -next_pair)]
+    pairs = [((z_at >> 1) + d) & 3 for d in (0, next_pair, -next_pair, 2)]
 
     def owner_of(block):
         return 2 * (16 * core + (block ^ 4)) + core
 
-    for half in range(2):
-        heads = [pairs[2 * half + (n >> 1)] + 4 * (n & 1) for n in range(4)]
-        wait("pos %d" % half, "lat %d" % half)
+    for n_pair in range(PAIRS):
+        heads = [pairs[n_pair], pairs[n_pair] + 4]
+        wait("pos %d" % n_pair, "lat %d" % n_pair)
         q_lat = jnp.concatenate(
             [
                 jnp.concatenate([lat[4 * h + j] for j in range(4)], axis=1)
@@ -369,7 +377,7 @@
             both = pos[h].astype(F32)
             q_pe += [both[:, :ROPE], both[:, ROPE:]]
         q_pe = jnp.concatenate(q_pe, axis=0).astype(BF16)
-        if half == 0:
+        if n_pair == 0:
             wait("cache", "share")
         scores = [
             (mm(q_lat, cache_v[n, :LAT]) + mm(q_pe, cache_v[n, LAT:])) * SCALE
@@ -383,8 +391,9 @@
         total = jnp.sum(weights[0], axis=1, keepdims=True) + jnp.sum(
             weights[1], axis=1, keepdims=True
         )
-        lane = lax.broadcasted_iota(jnp.int32, (128, 128), 1)
-        stats = jnp.where(lane == 0, top, jnp.where(lane == 1, total, 0.0)).T[:2]
+        lane = lax.broadcasted_iota(jnp.int32, (2 * ROWS, 128), 1)
+        stats = jnp.where(lane == 0, top, jnp.where(lane == 1, total, 0.0))
+        stats = jnp.concatenate([stats, stats], axis=0).T[:2]
         for n, h in enumerate(heads):
             ml_s[h] = stats if n == 0 else pltpu.roll(stats, 128 - 32 * n, 1)
 
@@ -523,12 +532,14 @@
     def send_part(i, carry):
         y = (group + far_first(i, GROUPS)) & (GROUPS - 1)
         for n in range(2):
-            send_or_keep(
-                part.at[n, y], part_r.at[2 * group + core], 9, me ^ n, y
-            )
+            send(part.at[n, y], part_r.at[2 * group + core], 9, me ^ n, y).start()
         return carry
 
-    lax.fori_loop(0, GROUPS, send_part, 0)
+    lax.fori_loop(0, GROUPS - 1, send_part, 0)
+    send(part.at[1, group], part_r.at[2 * group + core], 9, me ^ 1, group).start()
+    pltpu.make_async_copy(
+        part.at[0, group], part_r.at[2 * group + core], recv_sem.at[9]
+    ).start()
     arrives("part", part_r, 9)
     leaves("part out", part_r.at[pl.ds(0, 2 * GROUPS - 1)], 9)
     wait("part")
@@ -618,7 +629,7 @@
             pltpu.SemaphoreType.REGULAR,
             pltpu.SemaphoreType.DMA((13,)),
             pltpu.SemaphoreType.DMA((11,)),
-            pltpu.SemaphoreType.DMA((13,)),
+            pltpu.SemaphoreType.DMA((19,)),
         ],
         compiler_params=pltpu.CompilerParams(
             collective_id=0, has_side_effects=True, vmem_limit_bytes=60 * 2**20

time: 53.7 us -> 52.9 us (0.985)
  Pallas kernels: 52.3 us -> 51.5 us
    pallas_call x1, Pallas kernels: 52.3 us -> 51.5 us  [body(): pl.pallas_call(kernel, out_shape=jax.ShapeDtypeStruct((2, 2, WIDTH), BF16...]
where the time goes in v3:
time: 52.9 us; the launch traced here: 52.7 us
  Pallas kernels  51.5 us (97%)
  local copies, waits for them, and re-layouts  1.25 us (2%)
    pallas_call x1, Pallas kernels, body(): pl.pallas_call(kernel, out_shape=jax.ShapeDtypeStruct((2, 2, WIDTH), BF16...  51.5 us
    unnamed x1, local copies, waits for them, and re-layouts  1.25 us

profile of v3, /device:TPU:1, one launch (start us, length us, event | category | flops | bytes accessed | tf_op | source)
XLA Modules:
  0.0 52.7 jit_solution(7144860533307580193)
XLA Ops:
  0.0 51.5 %latent_attention.1 = bf16[2,2,112]{2,1,0:T(2,128)(2,1)} custom-call(bf16[32,1536]{1,0:T(8,128)(2,1)} %bitcast.18, bf16[32,576]{1,0:T(8,128)(2,1)} %bitcast.19, bf16[576,512]{1,0:T(8,128)(2,1)} %bitcast.12, bf16[48,1536]{1,0:T(8,128)(2,1)} %bitcast.17, bf16[16,8,128]{2,1,0:T(8,128)(2,1)} %bitcast.20, bf16[16,8,128]{2,1,0:T(8,128)(2,1)} %vup_hbm.1, ...), custom_call_target="tpu_custom_call" | custom-call | tf_op jit(solution)/shard_map/latent_attention/pallas_call | solution.py:591
  51.5 1.2 %copy.18 = bf16[2,2,112]{2,1,0:T(2,128)(2,1)} copy(bf16[2,2,112]{2,1,0:T(2,128)(2,1)} %latent_attention.1) | data formatting | bytes 1792

commit v4 on v3

--- a/solution.py
+++ b/solution.py
@@ -320,11 +320,30 @@
         send(lq_s, lat.at[slot], n, 2 * there + up_core, group, out=5).start()
         return carry
 
-    lax.fori_loop(0, CHIPS - 1, send_lat, 0)
+    def send_lat_far(i, carry):
+        z = (z_at + far_first(i, 8)) & 7
+        to = 16 * x_at + 2 * z + up_core
+        send(lq_s, lat.at[slot], 19, to, group, out=5).start()
+        return carry
+
+    lax.fori_loop(0, 3, send_lat_far, 0)
+    lax.fori_loop(12, CHIPS - 1, send_lat, 0)
     send_or_keep(lq_s, lat.at[slot], 11, 2 * chip + up_core, out=5)
-    leaves("lat out", lat, 5, core == up_core, lat.at[pl.ds(0, CHIPS - 1)])
-    for n in range(PAIRS):
-        arrives("lat %d" % n, lat.at[pl.ds(0, CHIPS // PAIRS)], 11 + 2 * n)
+    leaves("lat out", lat.at[pl.ds(0, 23)], 5, core == up_core, lat.at[pl.ds(0, 22)])
+    for n in range(2):
+        arrives("lat %d" % n, lat.at[pl.ds(0, 8)], 11 + 2 * n)
+    arrives("lat 3", lat.at[pl.ds(0, 6)], 17)
+    facing = (z_at & 1) == core
+    six = lat.at[pl.ds(0, 6)]
+    eight = lat.at[pl.ds(0, 8)]
+
+    def wait_beside():
+        pl.when(facing)(pltpu.make_async_copy(eight, eight, recv_sem.at[15]).wait)
+        pl.when(jnp.logical_not(facing))(
+            pltpu.make_async_copy(six, six, recv_sem.at[15]).wait
+        )
+
+    pending["lat 2"] = wait_beside
 
     share = send(cache_hbm, cache_v.at[1], 1, me ^ 1, group)
     share.start()
@@ -355,6 +374,23 @@
     leaves(
         "vw out", vw.at[pl.ds(0, CHIPS)], 3, owner, vw.at[pl.ds(0, CHIPS - 1)]
     )
+
+    def pass_on(*steps):
+        came = lat.at[pl.ds(0, 2 * len(steps))]
+        pltpu.make_async_copy(came, came, recv_sem.at[19]).wait()
+        for step in steps:
+            z = (z_at + step) & 7
+            for c in range(2):
+                made = 4 * ((2 * z + c) & 3) + (z >> 1)
+                row = (made & 7) * 4 + x_at
+                n = 11 + 2 * group_of(z_at, z >> 1)
+                for dx in (2, 1, 3):
+                    to = 16 * ((x_at + dx) & 3) + 2 * z_at + core
+                    send(lat.at[row], lat.at[row], n, to, group, out=11).start()
+
+    pl.when(facing)(lambda: pass_on(4))
+    pl.when(jnp.logical_not(facing))(lambda: pass_on(3, 5))
+    leaves("passed out", lat.at[pl.ds(0, 12)], 11, facing, lat.at[pl.ds(0, 6)])
 
     next_pair = 2 * (z_at & 1) - 1
     pairs = [((z_at >> 1) + d) & 3 for d in (0, next_pair, -next_pair, 2)]
@@ -504,15 +540,8 @@
     but_own = att.at[pl.ds(0, 15)]
     pl.when(owner)(pltpu.make_async_copy(but_own, but_own, recv_sem.at[8]).wait)
     pl.when(jnp.logical_not(owner))(all_here)
-    many = acc_r.at[0, pl.ds(0, 16)]
-
-    def all_sent():
-        def one(i, carry):
-            pltpu.make_async_copy(many, many, send_sem.at[8]).wait()
-            return carry
-
-        lax.fori_loop(0, CHIPS - 1, one, 0)
-
+    many = vw.at[pl.ds(0, CHIPS - 1)]
+    all_sent = pltpu.make_async_copy(many, many, send_sem.at[8]).wait
     pending["att out"] = lambda: pl.when(owner)(all_sent)
     rows = jnp.concatenate(
         [
@@ -540,6 +569,7 @@
     pltpu.make_async_copy(
         part.at[0, group], part_r.at[2 * group + core], recv_sem.at[9]
     ).start()
+    finish()
     arrives("part", part_r, 9)
     leaves("part out", part_r.at[pl.ds(0, 2 * GROUPS - 1)], 9)
     wait("part")
@@ -628,8 +658,8 @@
             vmem((2 * GROUPS, 4, 128), F32),
             pltpu.SemaphoreType.REGULAR,
             pltpu.SemaphoreType.DMA((13,)),
-            pltpu.SemaphoreType.DMA((11,)),
-            pltpu.SemaphoreType.DMA((19,)),
+            pltpu.SemaphoreType.DMA((12,)),
+            pltpu.SemaphoreType.DMA((20,)),
         ],
         compiler_params=pltpu.CompilerParams(
             collective_id=0, has_side_effects=True, vmem_limit_bytes=60 * 2**20

time: 52.9 us -> 50.6 us (0.957)
  Pallas kernels: 51.5 us -> 49.2 us
    pallas_call x1, Pallas kernels: 51.5 us -> 49.2 us  [body(): pl.pallas_call(kernel, out_shape=jax.ShapeDtypeStruct((2, 2, WIDTH), BF16...]
where the time goes in v4:
time: 50.6 us; the launch traced here: 50.4 us
  Pallas kernels  49.2 us (97%)
  local copies, waits for them, and re-layouts  1.25 us (2%)
    pallas_call x1, Pallas kernels, body(): pl.pallas_call(kernel, out_shape=jax.ShapeDtypeStruct((2, 2, WIDTH), BF16...  49.2 us
    unnamed x1, local copies, waits for them, and re-layouts  1.25 us

profile of v4, /device:TPU:1, one launch (start us, length us, event | category | flops | bytes accessed | tf_op | source)
XLA Modules:
  0.0 50.4 jit_solution(10200447213388625290)
XLA Ops:
  0.0 49.2 %latent_attention.1 = bf16[2,2,112]{2,1,0:T(2,128)(2,1)} custom-call(bf16[32,1536]{1,0:T(8,128)(2,1)} %bitcast.18, bf16[32,576]{1,0:T(8,128)(2,1)} %bitcast.19, bf16[576,512]{1,0:T(8,128)(2,1)} %bitcast.12, bf16[48,1536]{1,0:T(8,128)(2,1)} %bitcast.17, bf16[16,8,128]{2,1,0:T(8,128)(2,1)} %bitcast.20, bf16[16,8,128]{2,1,0:T(8,128)(2,1)} %vup_hbm.1, ...), custom_call_target="tpu_custom_call" | custom-call | tf_op jit(solution)/shard_map/latent_attention/pallas_call | solution.py:621
  49.2 1.2 %copy.18 = bf16[2,2,112]{2,1,0:T(2,128)(2,1)} copy(bf16[2,2,112]{2,1,0:T(2,128)(2,1)} %latent_attention.1) | data formatting | bytes 1792

commit v5 on v4

--- a/solution.py
+++ b/solution.py
@@ -349,12 +349,6 @@
     share.start()
     pending["share"] = share.wait_recv
     pending["share out"] = share.wait_send
-    share = send(
-        wo_hbm.at[:, pl.ds(other_col, HALF * NOPE)], wo_v.at[1], 10, me ^ 1, group
-    )
-    share.start()
-    pending["wo share"] = share.wait_recv
-    pending["wo share out"] = share.wait_send
 
     wait("vup", "avd")
     table = jnp.concatenate([avd_v[a].astype(F32) for a in range(8)], axis=1)
@@ -455,6 +449,13 @@
     leaves("ml out", ml_r.at[pl.ds(0, 16)], 6, owner, ml_r.at[pl.ds(0, 15)])
     arrives("acc", acc_r, 7, owner)
     leaves("acc out", acc_r.at[pl.ds(0, 16)], 7, owner, acc_r.at[pl.ds(0, 15)])
+
+    share = send(
+        wo_hbm.at[:, pl.ds(other_col, HALF * NOPE)], wo_v.at[1], 10, me ^ 1, group
+    )
+    share.start()
+    pending["wo share"] = share.wait_recv
+    pending["wo share out"] = share.wait_send
 
     wait("fresh", "avu")
     for name in ("vw", "ml", "acc"):

time: 50.6 us -> 50.6 us (level)
  no operation moved by 1% of the time
where the time goes in v5:
time: 50.6 us; the launch traced here: 50.4 us
  Pallas kernels  49.2 us (97%)
  local copies, waits for them, and re-layouts  1.25 us (2%)
    pallas_call x1, Pallas kernels, body(): pl.pallas_call(kernel, out_shape=jax.ShapeDtypeStruct((2, 2, WIDTH), BF16...  49.2 us
    unnamed x1, local copies, waits for them, and re-layouts  1.25 us

profile of v5, /device:TPU:1, one launch (start us, length us, event | category | flops | bytes accessed | tf_op | source)
XLA Modules:
  0.0 50.4 jit_solution(7269959363539189010)
XLA Ops:
  0.0 49.2 %latent_attention.1 = bf16[2,2,112]{2,1,0:T(2,128)(2,1)} custom-call(bf16[32,1536]{1,0:T(8,128)(2,1)} %bitcast.18, bf16[32,576]{1,0:T(8,128)(2,1)} %bitcast.19, bf16[576,512]{1,0:T(8,128)(2,1)} %bitcast.12, bf16[48,1536]{1,0:T(8,128)(2,1)} %bitcast.17, bf16[16,8,128]{2,1,0:T(8,128)(2,1)} %bitcast.20, bf16[16,8,128]{2,1,0:T(8,128)(2,1)} %vup_hbm.1, ...), custom_call_target="tpu_custom_call" | custom-call | tf_op jit(solution)/shard_map/latent_attention/pallas_call | solution.py:622
  49.2 1.2 %copy.18 = bf16[2,2,112]{2,1,0:T(2,128)(2,1)} copy(bf16[2,2,112]{2,1,0:T(2,128)(2,1)} %latent_attention.1) | data formatting | bytes 1792
